TPU v7x, 32 devices: a whole 2x2x4 slice. The times are simulated.
32 devices in a mesh: groups: 2 (over x), dp: 8 (over z, y), tensor: 2 (over core).
Axes of the slice: x: 2, y: 2, z: 4, core: 2. Of those that a mesh axis runs over, the one named last changes fastest.
Arguments:
- patches: bfloat16 [2048, 1280], P(('groups', 'dp')), parts along dimension 0, may hold values from -6 to 6
- image_tokens: int32 [16, 4], P(('groups', 'dp')), parts along dimension 0, may hold values from 1 to 16, 32 in all within a row
- vit_gain: float32 [1280], replicated, may hold values from 0.5 to 1.5
- vit_q: bfloat16 [1280, 1280], P(None, 'tensor'), may hold values from -0.15625 to 0.15625
- vit_k: bfloat16 [1280, 1280], P(None, 'tensor'), may hold values from -0.15625 to 0.15625
- vit_v: bfloat16 [1280, 1280], P(None, 'tensor'), may hold values from -0.15625 to 0.15625
- vit_out: bfloat16 [1280, 1280], P('tensor'), may hold values from -0.15625 to 0.15625
- merge_gain: float32 [1280], replicated, may hold values from 0.5 to 1.5
- merger_out: bfloat16 [5120, 8192], P('tensor', 'dp'), may hold values from -0.078125 to 0.078125
- text_rows: bfloat16 [2048, 8192], P(('groups', 'dp')), parts along dimension 0, may hold values from -6 to 6
- text_query: bfloat16 [2048, 4096], P(('groups', 'dp'), 'tensor'), parts along dimension 0, may hold values from -6 to 6
- text_seg: int32 [16, 128], P(('groups', 'dp')), parts along dimension 0, may hold values from 0 to 3, never falling along the last dimension, each value on 1 to 64 neighbouring positions
- vis_route: int32 [512, 1], P('groups'), parts along dimension 0, may hold values from 0 to 7; in each aligned block of 32 rows (0 to 31, 32 to 63, ...) at most 8 rows name the same one
- vis_seq: int32 [512], P('groups'), parts along dimension 0, may hold values from 0 to 3
- llm_gain: float32 [8192], replicated, may hold values from 0.5 to 1.5
- llm_k: bfloat16 [8192, 512], P('dp', 'tensor'), may hold values from -0.0625 to 0.0625
- llm_v: bfloat16 [8192, 512], P('dp', 'tensor'), may hold values from -0.0625 to 0.0625
Outputs:
- attended: bfloat16 [2048, 4096], P(('groups', 'dp'), 'tensor'), parts along dimension 0
There are 2 independent parts, one for each index of `groups`. A program takes and returns all parts, laid end to end along the dimension named above; an argument that names none is the same for every part. Nothing has to cross between parts.
Inputs may be any that keep to these rules, and one draw needn't show every extreme that they name: `image_tokens`: each row sums to 32, so the images of a block fill its 128 patch rows exactly. `text_seg`: within a row the sequence number never falls, and every one of the 4 sequences has a text token. `vis_route`: among the rows of one index of dp (aligned blocks of 32 rows) at most 8 name the same owner, a bound that some block reaches of them.
All inputs are finite; a program needn't handle non-finite values.
Results may differ from a plain program's by a relative error of at most 0.015.
Values may be sent and summed in bfloat16 or wider, within the bound.
A program may use at most 64 MiB of HBM per device.

v0:
```python
import math

import jax
import jax.numpy as jnp
from jax import lax
from jax.sharding import PartitionSpec as P

VHD = 80
QH = 32
KVH = 4
HD = 128


EPSILON = 1e-06
NEG_LARGE = -1e30


def layer_norm(values, scale_gain):
    values = values.astype(jnp.float32)
    centred = values - jnp.mean(values, axis=-1, keepdims=True)
    spread = jnp.mean(centred * centred, axis=-1, keepdims=True)
    return centred * lax.rsqrt(spread + EPSILON) * scale_gain


def rms_norm(values, scale_gain):
    values = values.astype(jnp.float32)
    power = jnp.mean(values * values, axis=-1, keepdims=True)
    return values * lax.rsqrt(power + EPSILON) * scale_gain


def image_index(counts, total):
    ends = 4 * jnp.cumsum(counts)
    positions = jnp.arange(total, dtype=jnp.int32)
    return jnp.sum((positions[:, None] >= ends[None, :]).astype(jnp.int32), axis=1)


def local_attention(query, keys, values, allowed, scale):
    scores = jnp.einsum("tagd,kad->agtk", query, keys, preferred_element_type=jnp.float32) * scale
    scores = jnp.where(allowed[None, None], scores, NEG_LARGE)
    weights = jax.nn.softmax(scores, axis=-1).astype(jnp.bfloat16)
    mixed = jnp.einsum("agtk,kad->tagd", weights, values, preferred_element_type=jnp.float32)
    return mixed.reshape(query.shape[0], -1).astype(jnp.bfloat16)


def head_split(inputs, weight, size):
    product = jnp.dot(inputs, weight, preferred_element_type=jnp.float32).astype(jnp.bfloat16)
    return product.reshape(inputs.shape[0], -1, size)


def add_product(inputs, piece):
    return jnp.dot(inputs, piece, preferred_element_type=jnp.float32)


def body(
    patches,
    image_tokens,
    vit_gain,
    vit_q,
    vit_k,
    vit_v,
    vit_out,
    merge_gain,
    merger_out,
    text_rows,
    text_query,
    text_seg,
    vis_route,
    vis_seq,
    llm_gain,
    llm_k,
    llm_v,
):
    total = patches.shape[0]
    width = patches.shape[1]
    image_of = image_index(image_tokens[0], total)
    same_image = image_of[:, None] == image_of[None, :]
    normed = layer_norm(patches, vit_gain).astype(jnp.bfloat16)
    vision_query = head_split(normed, vit_q, VHD)[:, :, None, :]
    vision_key = head_split(normed, vit_k, VHD)
    vision_value = head_split(normed, vit_v, VHD)
    attended = local_attention(
        vision_query, vision_key, vision_value, same_image, 1.0 / math.sqrt(VHD)
    )
    partial_mix = jnp.dot(attended, vit_out, preferred_element_type=jnp.float32)
    mixed_half = lax.psum_scatter(partial_mix, "tensor", scatter_dimension=0, tiled=True)
    half = mixed_half.shape[0]
    own_patches = lax.dynamic_slice_in_dim(patches, lax.axis_index("tensor") * half, half, 0)
    hidden = (own_patches.astype(jnp.float32) + mixed_half).astype(jnp.bfloat16)
    merged_half = layer_norm(hidden, merge_gain).astype(jnp.bfloat16).reshape(half // 4, 4 * width)
    merged = lax.all_gather(merged_half, "tensor", axis=0, tiled=True)
    feature_half = merger_out.shape[0]
    merged_cols = lax.dynamic_slice_in_dim(
        merged, lax.axis_index("tensor") * feature_half, feature_half, 1
    )
    merger_partial = jnp.dot(
        lax.all_gather(merged_cols, "dp", axis=0, tiled=True),
        merger_out,
        preferred_element_type=jnp.float32,
    )
    projected = lax.psum(merger_partial, "tensor").astype(jnp.bfloat16)
    projected_wide = projected.astype(jnp.float32)
    power = lax.psum(jnp.sum(projected_wide * projected_wide, axis=1), "dp")
    model_width = llm_gain.shape[0]
    block_cols = projected.shape[1]
    dp_index = lax.axis_index("dp")
    gain_block = lax.dynamic_slice_in_dim(llm_gain, dp_index * block_cols, block_cols, 0)
    visual_block = (
        projected_wide * lax.rsqrt(power / model_width + EPSILON)[:, None] * gain_block[None, :]
    ).astype(jnp.bfloat16)
    pair_weight = jnp.concatenate([llm_k, llm_v], axis=1)
    key_cols = llm_k.shape[1]
    devices = lax.axis_size("dp")
    owner_of = vis_route[:, 0]
    token_count = owner_of.shape[0]
    per_block = token_count // devices
    capacity = 2 * per_block // devices
    owner_slots = devices * capacity
    onehot = (
        (owner_of[:, None] == jnp.arange(devices, dtype=jnp.int32)[None, :])
        .astype(jnp.int32)
        .reshape(devices, per_block, devices)
    )
    rank = jnp.sum((jnp.cumsum(onehot, axis=1) - onehot) * onehot, axis=2).reshape(token_count)
    source = jnp.arange(token_count, dtype=jnp.int32) // per_block
    local_slot = source * capacity + rank
    mine = owner_of == dp_index
    slot_ids = jnp.arange(owner_slots, dtype=jnp.int32)
    hits = mine[None, :] & (slot_ids[:, None] == local_slot[None, :])
    visual_marker = jnp.sum(jnp.where(hits, (vis_seq + 1)[None, :], 0), axis=1)
    global_slot = owner_of * owner_slots + local_slot
    wanted = jnp.arange(owner_slots * lax.axis_size("dp"), dtype=jnp.int32)
    selector = (wanted[:, None] == global_slot[None, :]).astype(jnp.bfloat16)
    picked = jnp.dot(selector, visual_block, preferred_element_type=jnp.float32).astype(
        jnp.bfloat16
    )
    visual_pair = lax.psum_scatter(
        jnp.dot(picked, pair_weight, preferred_element_type=jnp.float32).astype(jnp.bfloat16),
        "dp",
        scatter_dimension=0,
        tiled=True,
    )
    visual_key = visual_pair[:, :key_cols]
    visual_value = visual_pair[:, key_cols:]
    text_in = rms_norm(text_rows, llm_gain).astype(jnp.bfloat16)
    text_count = text_in.shape[0]
    key_sum = add_product(text_in, lax.all_gather(llm_k, "dp", axis=0, tiled=True))
    value_sum = add_product(text_in, lax.all_gather(llm_v, "dp", axis=0, tiled=True))
    key_text = key_sum.astype(jnp.bfloat16)
    value_text = value_sum.astype(jnp.bfloat16)
    segment = text_seg[0]
    positions = jnp.arange(text_count, dtype=jnp.int32)
    text_allowed = (segment[:, None] == segment[None, :]) & (
        positions[None, :] <= positions[:, None]
    )
    visual_allowed = visual_marker[None, :] == (segment + 1)[:, None]
    allowed = jnp.concatenate([visual_allowed, text_allowed], axis=1)
    local_groups = key_cols // HD
    query_heads = text_query.reshape(text_count, local_groups, QH // KVH, HD)
    all_keys = jnp.concatenate([visual_key, key_text], axis=0).reshape(-1, local_groups, HD)
    all_values = jnp.concatenate([visual_value, value_text], axis=0).reshape(-1, local_groups, HD)
    return local_attention(query_heads, all_keys, all_values, allowed, 1.0 / math.sqrt(HD))


def solution(mesh):
    in_specs = (
        P(("groups", "dp"), None),
        P(("groups", "dp"), None),
        P(),
        P(None, "tensor"),
        P(None, "tensor"),
        P(None, "tensor"),
        P("tensor", None),
        P(),
        P("tensor", "dp"),
        P(("groups", "dp"), None),
        P(("groups", "dp"), "tensor"),
        P(("groups", "dp"), None),
        P("groups", None),
        P("groups"),
        P(),
        P("dp", "tensor"),
        P("dp", "tensor"),
    )
    out_specs = P(("groups", "dp"), "tensor")
    return jax.shard_map(body, mesh=mesh, in_specs=in_specs, out_specs=out_specs, check_vma=False)
```

profile of v0, /device:TPU:13, one launch (start us, length us, event | category | flops | bytes accessed | tf_op | source)
XLA Modules:
  0.0 327.8 jit_solution(13869202887388708500)
XLA Ops:
  6.5 1.2 convert_reduce_fusion
  7.8 1.2 fusion.19
  9.0 2.0 convolution_convert_fusion.4
  11.2 1.9 convolution_convert_fusion.3
  13.7 1.9 convolution_convert_fusion.5
  16.5 1.3 fusion.76
  17.8 10.0 %reduce-scatter.3.cloned.1.call-done = f32[64,1280]{1,0:T(8,128)} async-done(((f32[128,1280]{1,0:T(8,128)}), f32[64,1280]{1,0:T(8,128)}) %reduce-scatter.3.cloned.1.call-update) | async-done | bytes 327696 | tf_op jit(solution)/shard_map/reduce_scatter | solution.py:85
  27.9 1.1 convert_reduce_fusion.1
  29.5 2.0 all_gather.12
  34.5 38.0 %all-gather.4.cloned.1.call-done = bf16[256,2560]{1,0:T(8,128)(2,1)} async-done(((bf16[32,2560]{1,0:T(8,128)(2,1)}), bf16[256,2560]{1,0:T(8,128)(2,1)}) %all-gather.4.cloned.1.call-update) | async-done | bytes 1310736 | tf_op jit(solution)/shard_map/all_gather | solution.py:96
  72.5 4.4 %fusion.77 = f32[256,1024]{1,0:T(8,128)S(1)} fusion(bf16[256,2560]{1,0:T(8,128)(2,1)} %all-gather.4.cloned.1.call-done, bf16[2560,1024]{1,0:T(8,128)(2,1)} %param.25), kind=kOutput, calls=%fused_computation.105 | convolution fusion | flops 1342177280 | bytes 7602176 | tf_op jit(solution)/shard_map/dot_general | solution.py:95
  77.0 7.7 %all-reduce.1 = bf16[256,1024]{1,0:T(8,128)(2,1)S(1)} all-reduce(f32[256,1024]{1,0:T(8,128)S(1)} %fusion.77), channel_id=1, replica_groups=mesh['groups'=2,'dp'=8,'tensor'=2] {'tensor'}, use_global_device_ids=true, to_apply=%region_11.12 | all-reduce | flops 262144 | bytes 1572864 | tf_op jit(solution)/shard_map/psum | solution.py:100
  84.9 12.6 %psum.15 = f32[256]{0:T(256)S(1)} all-reduce(f32[256]{0:T(256)S(1)} %fusion.11), channel_id=1, replica_groups=mesh['groups'=2,'dp'=8,'tensor'=2] {'dp'}, use_global_device_ids=true, to_apply=%region_13.14 | all-reduce | flops 256 | bytes 2048 | tf_op jit(solution)/shard_map/psum | solution.py:102
  97.5 3.2 fusion.7
  102.4 2.1 fusion.1
  104.5 61.0 %reduce-scatter.5.cloned.1.call-done = bf16[64,512]{1,0:T(8,128)(2,1)} async-done(((bf16[512,512]{1,0:T(8,128)(2,1)}), bf16[64,512]{1,0:T(8,128)(2,1)}) %reduce-scatter.5.cloned.1.call-update) | async-done | bytes 65552 | tf_op jit(solution)/shard_map/reduce_scatter | solution.py:136
  165.5 0.8 fusion.67
  166.3 73.0 %all-gather.8.cloned.1.call-done = bf16[8192,256]{1,0:T(8,128)(2,1)} async-done(((bf16[1024,256]{1,0:T(8,128)(2,1)}), bf16[8192,256]{1,0:T(8,128)(2,1)}) %all-gather.8.cloned.1.call-update) | async-done | bytes 4194320 | tf_op jit(solution)/shard_map/all_gather | solution.py:146
  239.3 3.6 %convolution_convert_fusion.6 = bf16[128,256]{1,0:T(8,128)(2,1)S(1)} fusion(bf16[8192,256]{1,0:T(8,128)(2,1)} %all-gather.8.cloned.1.call-done, bf16[128,8192]{1,0:T(8,128)(2,1)} %param.26, f32[8192]{0:T(1024)S(1)} %copy-done.5, f32[128]{0:T(128)S(1)} %add_rsqrt_fusion.1), kind=kOutput, calls=%fused_computation.25 | convolution fusion | flops 541097984 | bytes 6390272 | tf_op jit(solution)/shard_map/dot_general | solution.py:51
  242.9 70.1 %all-gather.6.cloned.1.call-done = bf16[8192,256]{1,0:T(8,128)(2,1)} async-done(((bf16[1024,256]{1,0:T(8,128)(2,1)}), bf16[8192,256]{1,0:T(8,128)(2,1)}) %all-gather.6.cloned.1.call-update) | async-done | bytes 4194320 | tf_op jit(solution)/shard_map/all_gather | solution.py:147
  313.0 3.6 %convolution_convert_fusion.7 = bf16[128,256]{1,0:T(8,128)(2,1)S(1)} fusion(bf16[8192,256]{1,0:T(8,128)(2,1)} %all-gather.6.cloned.1.call-done, bf16[128,8192]{1,0:T(8,128)(2,1)} %param.26, f32[8192]{0:T(1024)S(1)} %copy-done.5, f32[128]{0:T(128)S(1)} %add_rsqrt_fusion.1), kind=kOutput, calls=%fused_computation.26 | convolution fusion | flops 541097984 | bytes 6390272 | tf_op jit(solution)/shard_map/dot_general | solution.py:51
  316.7 1.8 fusion.71
  318.5 1.8 convolution_convert_fusion.1
  320.2 1.0 copy.64
  (72 shorter events, 6.9 us)
Async XLA Ops:
  6.5 9.9 %copy-start = (bf16[640,1280]{1,0:T(8,128)(2,1)S(1)}, bf16[640,1280]{1,0:T(8,128)(2,1)}, u32[]{:S(2)}) copy-start(bf16[640,1280]{1,0:T(8,128)(2,1)} %param.23) | copy-start | bytes 4915204
  6.5 4.7 %copy-start.1 = (bf16[128,1280]{1,0:T(8,128)(2,1)S(1)}, bf16[128,1280]{1,0:T(8,128)(2,1)}, u32[]{:S(2)}) copy-start(bf16[128,1280]{1,0:T(8,128)(2,1)} %param.17) | copy-start | bytes 983044
  6.5 4.7 %copy-start.8 = (f32[1280]{0:T(1024)S(1)}, f32[1280]{0:T(1024)}, u32[]{:S(2)}) copy-start(f32[1280]{0:T(1024)} %param.19) | copy-start | bytes 15364
  6.5 21.3 %reduce-scatter.3.cloned.1.call-start = ((), (), s32[]{:S(2)}) async-start(), calls=%async_computation.2 | async-start | bytes 983040 | tf_op jit(solution)/shard_map/reduce_scatter | solution.py:85
  9.0 4.3 %copy-start.9 = (s32[1,4]{1,0:T(1,128)S(1)}, s32[1,4]{1,0:T(1,128)}, u32[]{:S(2)}) copy-start(s32[1,4]{1,0:T(1,128)} %param.18) | copy-start | bytes 52
  16.4 12.8 %copy-start.3 = (f32[1280]{0:T(1024)S(1)}, f32[1280]{0:T(1024)}, u32[]{:S(2)}) copy-start(f32[1280]{0:T(1024)} %param.24) | copy-start | bytes 15364
  17.8 15.1 %copy-start.4 = (s32[256,1]{0,1:T(1,128)S(1)}, s32[256,1]{0,1:T(1,128)}, u32[]{:S(2)}) copy-start(s32[256,1]{0,1:T(1,128)} %param.29) | copy-start | bytes 3076
  17.8 54.8 %all-gather.4.cloned.1.call-start = ((), (), s32[]{:S(2)}) async-start(), calls=%async_computation.3 | async-start | bytes 1474560 | tf_op jit(solution)/shard_map/all_gather | solution.py:96
  32.2 133.3 %reduce-scatter.5.cloned.1.call-start = ((), (), s32[]{:S(2)}) async-start(), calls=%async_computation.4 | async-start | bytes 589824 | tf_op jit(solution)/shard_map/reduce_scatter | solution.py:136
  77.0 20.5 %dynamic-slice-start = ((f32[8192]{0:T(1024)}, s32[]{:T(128)}), f32[1024]{0:T(1024)S(1)}, s32[]{:S(2)}) async-start(f32[8192]{0:T(1024)} %param.31, s32[]{:T(128)} %select_n.37), calls=%async_computation.7 | async-start | bytes 8704 | tf_op jit(solution)/shard_map/dynamic_slice | solution.py:106
  97.5 4.4 %copy-start.2 = (bf16[128,2048]{1,0:T(8,128)(2,1)S(1)}, bf16[128,2048]{1,0:T(8,128)(2,1)}, u32[]{:S(2)}) copy-start(bf16[128,2048]{1,0:T(8,128)(2,1)} %param.27) | copy-start | bytes 1572868
  100.7 1.4 copy-start.7
  100.7 1.5 copy-start.6
  100.7 138.6 %copy-start.5 = (f32[8192]{0:T(1024)S(1)}, f32[8192]{0:T(1024)}, u32[]{:S(2)}) copy-start(f32[8192]{0:T(1024)} %param.31) | copy-start | bytes 98308
  100.7 138.6 %all-gather.8.cloned.1.call-start = ((), (), s32[]{:S(2)}) async-start(), calls=%async_computation.6 | async-start | bytes 4718592 | tf_op jit(solution)/shard_map/all_gather | solution.py:146
  101.3 211.7 %all-gather.6.cloned.1.call-start = ((), (), s32[]{:S(2)}) async-start(), calls=%async_computation.5 | async-start | bytes 4718592 | tf_op jit(solution)/shard_map/all_gather | solution.py:147
Sparse Core Ops, SparseCore 0:
  17.9 9.9 reduce-scatter.2
  32.4 40.1 all-gather.3
  100.8 64.6 reduce-scatter.4
  167.5 71.8 all-gather.7
  241.3 71.6 all-gather.5
where the time goes:
time: 332 us; the launch traced here: 328 us
  waiting for transfers between devices  253 us (76%)
  matrix products  26 us (8%)
  blocking collectives  22.4 us (7%)
  between operations  13.4 us (4%)
  other arithmetic  8.36 us (3%)
  local copies, waits for them, and re-layouts  4.15 us (1%)
    all_gather x1, waiting for transfers between devices, body(): lax.all_gather(llm_k, 'dp', axis=0, tiled=True)  73 us
    all_gather x1, waiting for transfers between devices, body(): lax.all_gather(llm_v, 'dp', axis=0, tiled=True)  70.1 us
    reduce_scatter x1, waiting for transfers between devices, body(): lax.psum_scatter(jnp.dot(picked, pair_weight, preferred_element_type=jnp....  61 us
    all_gather x1, waiting for transfers between devices, body(): lax.all_gather(merged_cols, 'dp', axis=0, tiled=True)  38 us
    psum x1, blocking collectives, body(): power = lax.psum(jnp.sum(projected_wide * projected_wide, axis=1), 'dp')  12.6 us
    reduce_scatter x1, waiting for transfers between devices, body(): lax.psum_scatter(partial_mix, 'tensor', scatter_dimension=0, tiled=True)  10 us
    psum x1, blocking collectives, body(): projected = lax.psum(merger_partial, 'tensor').astype(jnp.bfloat16)  7.73 us
    dot_general x2, matrix products, add_product(): return jnp.dot(inputs, piece, preferred_element_type=jnp.float32)  7.17 us
  transfers between devices with their start and end apart: 5, of which 5 were waited for; matrix products, arithmetic and copies ran while one was open for 3% of the time, Pallas kernels for 0%

commit v1 on v0

v1 whole, which is shorter than its diff:
```python
import functools
import math

import jax
import jax.numpy as jnp
from jax import lax
from jax.experimental import pallas as pl
from jax.experimental.pallas import tpu as pltpu
from jax.sharding import PartitionSpec as P

VHD = 80
QH = 32
KVH = 4
HD = 128


EPSILON = 1e-06
NEG_LARGE = -1e30


def layer_norm(values, scale_gain):
    values = values.astype(jnp.float32)
    centred = values - jnp.mean(values, axis=-1, keepdims=True)
    spread = jnp.mean(centred * centred, axis=-1, keepdims=True)
    return centred * lax.rsqrt(spread + EPSILON) * scale_gain


def rms_norm(values, scale_gain):
    values = values.astype(jnp.float32)
    power = jnp.mean(values * values, axis=-1, keepdims=True)
    return values * lax.rsqrt(power + EPSILON) * scale_gain


def image_index(counts, total):
    ends = 4 * jnp.cumsum(counts)
    positions = jnp.arange(total, dtype=jnp.int32)
    return jnp.sum((positions[:, None] >= ends[None, :]).astype(jnp.int32), axis=1)


def local_attention(query, keys, values, allowed, scale):
    scores = jnp.einsum("tagd,kad->agtk", query, keys, preferred_element_type=jnp.float32) * scale
    scores = jnp.where(allowed[None, None], scores, NEG_LARGE)
    weights = jax.nn.softmax(scores, axis=-1).astype(jnp.bfloat16)
    mixed = jnp.einsum("agtk,kad->tagd", weights, values, preferred_element_type=jnp.float32)
    return mixed.reshape(query.shape[0], -1).astype(jnp.bfloat16)


MESH = pl.DeviceIdType.MESH
MARK = 128


def dot32(left, right):
    return jnp.dot(left, right, preferred_element_type=jnp.float32)


def kernel(
    n,
    patches,
    image_col,
    image_row,
    vit_gain,
    vit_q_hbm,
    vit_k_hbm,
    vit_v_hbm,
    vit_out_hbm,
    merge_gain,
    merger_hbm,
    text_hbm,
    selector,
    llm_gain,
    llm_k_hbm,
    llm_v_hbm,
    out,
    wq,
    wk,
    wv,
    wo,
    merger,
    pair_weight,
    text,
    text_in,
    text_buf,
    query,
    keys,
    values,
    mixed,
    mix,
    mix_recv,
    merged,
    part,
    part_recv,
    text_send,
    text_recv,
    vis_send,
    vis_recv,
    load_sem,
    text_sems,
    forward_sems,
    mix_sems,
    merged_sems,
    part_sems,
    text_back_sems,
    vis_back_sems,
):
    me = lax.axis_index("dp")
    core = lax.axis_index("tensor")
    other = 1 - core
    rows = text_buf.shape[1]
    text_half = rows // 2
    cols = text_buf.shape[2]
    width = llm_gain.shape[1]
    sibling = {"tensor": other}
    kv = llm_k_hbm.shape[1]

    def ahead(step):
        return lax.rem(me + step, n)

    def behind(step):
        return lax.rem(me + n - step, n)

    mine = pl.ds(pl.multiple_of(core * text_half, text_half), text_half)
    theirs = pl.ds(pl.multiple_of(other * text_half, text_half), text_half)
    loads = [
        pltpu.make_async_copy(source, target, load_sem.at[i])
        for i, (source, target) in enumerate(
            [
                (text_hbm.at[mine], text),
                (vit_q_hbm, wq),
                (vit_k_hbm, wk),
                (vit_v_hbm, wv),
                (vit_out_hbm, wo),
                (llm_k_hbm, pair_weight.at[:, 0:kv]),
                (llm_v_hbm, pair_weight.at[:, kv : 2 * kv]),
                (merger_hbm, merger),
            ]
        )
    ]
    for load in loads:
        load.start()

    barrier = pltpu.get_barrier_semaphore()

    def greet(step, carry):
        pl.semaphore_signal(barrier, inc=1, device_id={"dp": ahead(step)}, device_id_type=MESH)
        return carry

    lax.fori_loop(1, n, greet, 0)
    pl.semaphore_signal(barrier, inc=1, device_id=sibling, device_id_type=MESH)

    def remote(source, target, send, recv, device):
        return pltpu.make_async_remote_copy(
            src_ref=source,
            dst_ref=target,
            send_sem=send,
            recv_sem=recv,
            device_id=device,
            device_id_type=MESH,
        )

    def text_copy(step):
        start = pl.multiple_of(ahead(step) * cols, cols)
        return remote(
            text_in.at[:, pl.ds(start, cols)],
            text_buf.at[step, mine],
            text_sems.at[0, step],
            text_sems.at[1, step],
            {"dp": ahead(step)},
        )

    def forward_copy(step):
        return remote(
            text_buf.at[step, mine],
            text_buf.at[step, mine],
            forward_sems.at[0, step],
            forward_sems.at[1, step],
            sibling,
        )

    def merged_copy(step):
        return remote(
            merged.at[0],
            merged.at[step],
            merged_sems.at[0, step],
            merged_sems.at[1, step],
            {"dp": ahead(step)},
        )

    def text_back(step):
        return remote(
            text_send.at[step],
            text_recv.at[step],
            text_back_sems.at[0, step],
            text_back_sems.at[1, step],
            {"dp": behind(step)},
        )

    def vis_back(step):
        return remote(
            vis_send.at[step],
            vis_recv.at[step],
            vis_back_sems.at[0, step],
            vis_back_sems.at[1, step],
            {"dp": ahead(step)},
        )

    def each(first, act):
        def run(step, carry):
            act(step)
            return carry

        lax.fori_loop(first, n, run, 0)

    loads[0].wait()

    def norm_rows(i, carry):
        at = pl.ds(pl.multiple_of(i * 16, 16), 16)
        text_in[at, :] = rms_norm(text[at, :], llm_gain[...]).astype(jnp.bfloat16)
        return carry

    lax.fori_loop(0, text_half // 16, norm_rows, 0)
    own_cols = pl.ds(pl.multiple_of(me * cols, cols), cols)
    text_buf[0, mine, :] = text_in[:, own_cols]
    pl.semaphore_wait(barrier, n)
    each(1, lambda step: text_copy(step).start())
    forward_copy(0).start()

    normed = layer_norm(patches[...], vit_gain[...]).astype(jnp.bfloat16)
    for load, weight, place in zip(loads[1:4], (wq, wk, wv), (query, keys, values)):
        load.wait()
        place[...] = dot32(normed, weight[...]).astype(jnp.bfloat16)
    same = image_col[...] == image_row[...]
    mixed[...] = jnp.zeros_like(mixed)
    for head in range(query.shape[1] // VHD):
        low = head * VHD
        base = low // 128 * 128
        end = -(-(low + VHD) // 128) * 128
        lane = lax.broadcasted_iota(jnp.int32, (query.shape[0], end - base), 1)
        inside = (lane >= low - base) & (lane < low - base + VHD)
        q = jnp.where(inside, query[:, base:end].astype(jnp.float32), 0.0).astype(jnp.bfloat16)
        v = jnp.where(inside, values[:, base:end].astype(jnp.float32), 0.0).astype(jnp.bfloat16)
        scores = lax.dot_general(
            q, keys[:, base:end], (((1,), (1,)), ((), ())), preferred_element_type=jnp.float32
        ) * (1.0 / math.sqrt(VHD))
        scores = jnp.where(same, scores, NEG_LARGE)
        scores = jnp.exp(scores - jnp.max(scores, axis=1, keepdims=True))
        weights = (scores / jnp.sum(scores, axis=1, keepdims=True)).astype(jnp.bfloat16)
        mixed[:, base:end] += dot32(weights, v)
    loads[4].wait()
    mix[...] = dot32(mixed[...].astype(jnp.bfloat16), wo[...])
    half = mix.shape[0] // 2
    own_half = pl.ds(pl.multiple_of(core * half, half), half)
    other_half = pl.ds(pl.multiple_of(other * half, half), half)
    swap = remote(mix.at[other_half], mix_recv, mix_sems.at[0], mix_sems.at[1], sibling)
    swap.start()
    swap.wait()
    hidden = (patches[own_half, :].astype(jnp.float32) + (mix[own_half, :] + mix_recv[...])).astype(
        jnp.bfloat16
    )
    normal = layer_norm(hidden, merge_gain[...]).astype(jnp.bfloat16)
    vision_width = normal.shape[1]
    merged[0, :, 0:vision_width] = normal[: half // 2]
    merged[0, :, vision_width : 2 * vision_width] = normal[half // 2 :]
    each(1, lambda step: merged_copy(step).start())

    def hand_over(step):
        text_copy(step).wait_recv()
        forward_copy(step).start()

    each(1, hand_over)
    loads[5].wait()
    loads[6].wait()

    def project_text(step):
        forward_copy(step).wait_recv()
        text_send[step] = dot32(text_buf[step], pair_weight[...]).astype(jnp.bfloat16)

    project_text(0)

    def project_and_send(step):
        project_text(step)
        text_back(step).start()

    each(1, project_and_send)

    loads[7].wait()
    each(1, lambda step: merged_copy(step).wait_recv())
    gathered = merged[...].reshape(-1, merged.shape[2])
    block = 256

    def part_copy(i):
        at = pl.ds(pl.multiple_of(i * block, block), block)
        return remote(
            part.at[:, at], part_recv.at[:, at], part_sems.at[0, i], part_sems.at[1, i], sibling
        )

    for i in range(cols // block):
        at = slice(i * block, (i + 1) * block)
        part[:, at] = dot32(gathered, merger[:, at])
        part_copy(i).start()
    tokens = part.shape[0]
    power = jnp.zeros((tokens, 1), jnp.float32)
    pair = jnp.zeros((tokens, 2 * kv), jnp.float32)
    for i in range(cols // block):
        at = slice(i * block, (i + 1) * block)
        part_copy(i).wait_recv()
        wide = (part[:, at] + part_recv[:, at]).astype(jnp.bfloat16).astype(jnp.float32)
        power = power + jnp.sum(wide * wide, axis=1, keepdims=True)
        gain = llm_gain[:, pl.ds(pl.multiple_of(me * cols + i * block, block), block)]
        pair = pair + dot32((wide * gain).astype(jnp.bfloat16), pair_weight[at, :])
    coarse = power.astype(jnp.bfloat16).astype(jnp.float32)
    lane = lax.broadcasted_iota(jnp.int32, (tokens, MARK), 1)
    marks = jnp.where(lane < MARK // 2, coarse, power - coarse)
    row = jnp.concatenate([pair.astype(jnp.bfloat16), marks.astype(jnp.bfloat16)], axis=1)

    def route(step):
        vis_send[step] = dot32(selector[step], row).astype(jnp.bfloat16)

    route(0)

    def route_and_send(step):
        route(step)
        vis_back(step).start()

    each(1, route_and_send)

    slots = vis_send.shape[1]

    def add_text(step, total):
        text_back(step).wait_recv()
        return total + text_recv[step].astype(jnp.float32)

    out[slots:, :] = lax.fori_loop(1, n, add_text, text_send[0].astype(jnp.float32)).astype(
        jnp.bfloat16
    )

    def add_visual(step, total):
        vis_back(step).wait_recv()
        return total + vis_recv[step].astype(jnp.float32)

    total = lax.fori_loop(1, n, add_visual, vis_send[0].astype(jnp.float32))
    squares = jnp.sum(total[:, 2 * kv :], axis=1, keepdims=True) * (2.0 / MARK)
    out[:slots, :] = (total[:, : 2 * kv] * lax.rsqrt(squares / width + EPSILON)).astype(jnp.bfloat16)

    each(0, lambda step: forward_copy(step).wait_send())
    for i in range(cols // block):
        part_copy(i).wait_send()

    def drain(step):
        text_copy(step).wait_send()
        merged_copy(step).wait_send()
        text_back(step).wait_send()
        vis_back(step).wait_send()

    each(1, drain)


def body(
    patches,
    image_tokens,
    vit_gain,
    vit_q,
    vit_k,
    vit_v,
    vit_out,
    merge_gain,
    merger_out,
    text_rows,
    text_query,
    text_seg,
    vis_route,
    vis_seq,
    llm_gain,
    llm_k,
    llm_v,
):
    devices = lax.axis_size("dp")
    dp_index = lax.axis_index("dp")
    total, width = patches.shape
    ordered = patches.reshape(total // 4, 4, width).transpose(1, 0, 2).reshape(total, width)
    image_of = image_index(image_tokens[0], total).reshape(total // 4, 4).T.reshape(total)
    key_cols = llm_k.shape[1]
    owner_of = vis_route[:, 0]
    token_count = owner_of.shape[0]
    per_block = token_count // devices
    capacity = 2 * per_block // devices
    owner_slots = devices * capacity
    ids = jnp.arange(devices, dtype=jnp.int32)
    owners = owner_of.reshape(devices, per_block)
    earlier = jnp.arange(per_block)[None, :] < jnp.arange(per_block)[:, None]
    alike = (owners[:, :, None] == owners[:, None, :]) & earlier[None]
    rank = jnp.sum(alike.astype(jnp.int32), axis=2)
    local_slot = ids[:, None] * capacity + rank
    slot_ids = jnp.arange(owner_slots, dtype=jnp.int32)
    hits = (owner_of == dp_index)[None, :] & (slot_ids[:, None] == local_slot.reshape(-1)[None, :])
    visual_marker = jnp.sum(jnp.where(hits, (vis_seq + 1)[None, :], 0), axis=1)
    source = (dp_index - ids) % devices
    turned_owner = jnp.sum(
        jnp.where(source[:, None, None] == ids[None, :, None], owners[None], 0), axis=1
    ).reshape(-1)
    turned_slot = jnp.sum(
        jnp.where(source[:, None, None] == ids[None, :, None], local_slot[None], 0), axis=1
    ).reshape(-1)
    target = (dp_index + ids) % devices
    selector = (
        (turned_owner[None, None, :] == target[:, None, None])
        & (turned_slot[None, None, :] == slot_ids[None, :, None])
    ).astype(jnp.bfloat16)

    text_count, model_width = text_rows.shape
    cols = merger_out.shape[1]
    half = total // 2
    vmem = pl.BlockSpec(memory_space=pltpu.VMEM)
    hbm = pl.BlockSpec(memory_space=pl.ANY)
    bf16, f32 = jnp.bfloat16, jnp.float32
    dma = pltpu.SemaphoreType.DMA
    pair = pl.pallas_call(
        functools.partial(kernel, devices),
        out_shape=jax.ShapeDtypeStruct((owner_slots + text_count, 2 * key_cols), bf16),
        in_specs=[vmem] * 4 + [hbm] * 4 + [vmem, hbm, hbm, vmem, vmem, hbm, hbm],
        out_specs=vmem,
        scratch_shapes=[
            pltpu.VMEM(vit_q.shape, bf16),
            pltpu.VMEM(vit_k.shape, bf16),
            pltpu.VMEM(vit_v.shape, bf16),
            pltpu.VMEM(vit_out.shape, bf16),
            pltpu.VMEM(merger_out.shape, bf16),
            pltpu.VMEM((cols, 2 * key_cols), bf16),
            pltpu.VMEM((text_count // 2, model_width), bf16),
            pltpu.VMEM((text_count // 2, model_width), bf16),
            pltpu.VMEM((devices, text_count, cols), bf16),
            pltpu.VMEM((total, vit_q.shape[1]), bf16),
            pltpu.VMEM((total, vit_q.shape[1]), bf16),
            pltpu.VMEM((total, vit_q.shape[1]), bf16),
            pltpu.VMEM((total, vit_q.shape[1]), f32),
            pltpu.VMEM((total, width), f32),
            pltpu.VMEM((half, width), f32),
            pltpu.VMEM((devices, half // 2, 2 * width), bf16),
            pltpu.VMEM((token_count, cols), f32),
            pltpu.VMEM((token_count, cols), f32),
            pltpu.VMEM((devices, text_count, 2 * key_cols), bf16),
            pltpu.VMEM((devices, text_count, 2 * key_cols), bf16),
            pltpu.VMEM((devices, owner_slots, 2 * key_cols + MARK), bf16),
            pltpu.VMEM((devices, owner_slots, 2 * key_cols + MARK), bf16),
            dma((8,)),
            dma((2, devices)),
            dma((2, devices)),
            dma((2,)),
            dma((2, devices)),
            dma((2, cols // 256)),
            dma((2, devices)),
            dma((2, devices)),
        ],
        compiler_params=pltpu.CompilerParams(
            collective_id=0, has_side_effects=True, vmem_limit_bytes=56 * 1024 * 1024
        ),
    )(
        ordered,
        image_of[:, None],
        image_of[None, :],
        vit_gain[None],
        vit_q,
        vit_k,
        vit_v,
        vit_out,
        merge_gain[None],
        merger_out,
        text_rows,
        selector,
        llm_gain[None],
        llm_k,
        llm_v,
    )
    segment = text_seg[0]
    positions = jnp.arange(text_count, dtype=jnp.int32)
    text_allowed = (segment[:, None] == segment[None, :]) & (
        positions[None, :] <= positions[:, None]
    )
    visual_allowed = visual_marker[None, :] == (segment + 1)[:, None]
    allowed = jnp.concatenate([visual_allowed, text_allowed], axis=1)
    local_groups = key_cols // HD
    query_heads = text_query.reshape(text_count, local_groups, QH // KVH, HD)
    all_keys = pair[:, :key_cols].reshape(-1, local_groups, HD)
    all_values = pair[:, key_cols:].reshape(-1, local_groups, HD)
    return local_attention(query_heads, all_keys, all_values, allowed, 1.0 / math.sqrt(HD))


def solution(mesh):
    in_specs = (
        P(("groups", "dp"), None),
        P(("groups", "dp"), None),
        P(),
        P(None, "tensor"),
        P(None, "tensor"),
        P(None, "tensor"),
        P("tensor", None),
        P(),
        P("tensor", "dp"),
        P(("groups", "dp"), None),
        P(("groups", "dp"), "tensor"),
        P(("groups", "dp"), None),
        P("groups", None),
        P("groups"),
        P(),
        P("dp", "tensor"),
        P("dp", "tensor"),
    )
    out_specs = P(("groups", "dp"), "tensor")
    return jax.shard_map(body, mesh=mesh, in_specs=in_specs, out_specs=out_specs, check_vma=False)
```

time: 332 us -> 113 us (0.34)
  waiting for transfers between devices: 253 us -> 0 us
  Pallas kernels: 0 us -> 94.4 us
  matrix products: 26 us -> 1.01 us
  blocking collectives: 22.4 us -> 0 us
  between operations: 13.4 us -> 0.1 us
  local copies, waits for them, and re-layouts: 4.15 us -> 8.93 us
    all_gather x3 -> x0, waiting for transfers between devices: 181 us -> none  [the longest x1 73 us: body(): lax.all_gather(llm_k, 'dp', axis=0, tiled=True)]
    pallas_call x0 -> x1, Pallas kernels: none -> 94.4 us  [body(): pl.pallas_call(functools.partial(kernel, devices), out_shape=jax.ShapeDty...]
    reduce_scatter x2 -> x0, waiting for transfers between devices: 71.1 us -> none  [the longest x1 61 us: body(): lax.psum_scatter(jnp.dot(picked, pair_weight, preferred_element_type=jnp....]
    dot_general x9 -> x0, matrix products: 22.2 us -> none  [the longest x2 7.17 us: add_product(): return jnp.dot(inputs, piece, preferred_element_type=jnp.float32)]
    psum x2 -> x0, blocking collectives: 20.3 us -> none  [the longest x1 12.6 us: body(): power = lax.psum(jnp.sum(projected_wide * projected_wide, axis=1), 'dp')]
    reduce_sum x7 -> x2, other arithmetic: 6.12 us -> 0.4 us  [the longest x1 0.3 us: body(): rank = jnp.sum(alike.astype(jnp.int32), axis=2)]
  transfers between devices with their start and end apart: 5 -> 0, of which waited for: 5 -> 0; matrix products, arithmetic and copies ran while one was open for 3% -> 0% of each run, Pallas kernels for 0% -> 0%
where the time goes in v1:
time: 113 us; the launch traced here: 111 us
  Pallas kernels  94.4 us (84%)
  local copies, waits for them, and re-layouts  8.93 us (8%)
  other arithmetic  6.7 us (6%)
    pallas_call x1, Pallas kernels, body(): pl.pallas_call(functools.partial(kernel, devices), out_shape=jax.ShapeDty...  94.4 us

profile of v1, /device:TPU:13, one launch (start us, length us, event | category | flops | bytes accessed | tf_op | source)
XLA Modules:
  0.0 111.2 jit_solution(3765964178384193923)
XLA Ops:
  0.0 0.8 reduce-window.8
  0.9 0.7 broadcast_add_fusion.2
  1.6 0.7 compare_reduce_fusion
  2.3 0.5 broadcast.161
  2.8 1.3 %reduce.5 = s32[256]{0:T(256)S(1)} reduce(s32[256,1]{0,1:T(1,128)} %param.29, s32[]{:T(128)} %broadcast.161), dimensions={1}, to_apply=%param.29.reduce_sub_computation.3 | reduce | bytes 2052 | tf_op args[12]
  4.2 0.7 broadcast_add_fusion.1
  5.0 0.3 convert_reduce_fusion
  5.4 0.1 select_reduce_fusion
  5.6 0.1 select_reduce_fusion.2
  5.9 1.3 %broadcast_in_dim.87.vit_gain = f32[1,1280]{1,0:T(1,128)} reshape(f32[1280]{0:T(1024)} %param.19) | data formatting | bytes 10240 | tf_op jit(solution)/shard_map/broadcast_in_dim | solution.py:460
  7.2 1.3 %broadcast_in_dim.88.merge_gain = f32[1,1280]{1,0:T(1,128)} reshape(f32[1280]{0:T(1024)} %param.24) | data formatting | bytes 10240 | tf_op jit(solution)/shard_map/broadcast_in_dim | solution.py:465
  8.6 0.1 reshape.229
  8.8 0.7 broadcast_in_dim_reshape.10.image_row
  9.4 0.8 fusion.16
  10.3 0.7 broadcast_in_dim_reshape.11.image_col
  11.0 0.7 and_convert_fusion.selector
  11.7 1.1 reshape.226
  12.8 0.8 copy.34
  13.6 94.4 %shard_map.163 = bf16[192,512]{1,0:T(8,128)(2,1)} custom-call(bf16[128,1280]{1,0:T(8,128)(2,1)} %bitcast.27, s32[128,1]{1,0:T(8,128)} %broadcast_in_dim_reshape.11.image_col, s32[1,128]{1,0:T(1,128)} %broadcast_in_dim_reshape.10.image_row, f32[1,1280]{1,0:T(1,128)} %broadcast_in_dim.87.vit_gain, bf16[1280,640]{1,0:T(8,128)(2,1)} %vit_q_hbm.1, ...), custom_call_target="tpu_custom_call" | custom-call | tf_op jit(solution)/shard_map/pallas_call | solution.py:416
  108.0 1.0 fusion.21
  109.0 0.1 copy.48
  109.2 0.6 fusion.22
  109.8 0.4 convolution_convert_fusion
  110.2 1.0 copy.41
  (20 shorter events, 0.9 us)
Async XLA Ops:
  13.6 95.5 %copy-start = (bf16[128,2048]{1,0:T(8,128)(2,1)S(1)}, bf16[128,2048]{1,0:T(8,128)(2,1)}, u32[]{:S(2)}) copy-start(bf16[128,2048]{1,0:T(8,128)(2,1)} %param.27) | copy-start | bytes 1572868

commit v2 on v1

--- a/solution.py
+++ b/solution.py
@@ -31,12 +31,6 @@
     return values * lax.rsqrt(power + EPSILON) * scale_gain
 
 
-def image_index(counts, total):
-    ends = 4 * jnp.cumsum(counts)
-    positions = jnp.arange(total, dtype=jnp.int32)
-    return jnp.sum((positions[:, None] >= ends[None, :]).astype(jnp.int32), axis=1)
-
-
 def local_attention(query, keys, values, allowed, scale):
     scores = jnp.einsum("tagd,kad->agtk", query, keys, preferred_element_type=jnp.float32) * scale
     scores = jnp.where(allowed[None, None], scores, NEG_LARGE)
@@ -56,8 +50,7 @@
 def kernel(
     n,
     patches,
-    image_col,
-    image_row,
+    image_tokens,
     vit_gain,
     vit_q_hbm,
     vit_k_hbm,
@@ -66,11 +59,16 @@
     merge_gain,
     merger_hbm,
     text_hbm,
-    selector,
-    llm_gain,
+    route,
+    vis_seq,
+    llm_gain_flat,
     llm_k_hbm,
     llm_v_hbm,
     out,
+    marker,
+    code,
+    llm_gain,
+    ordered,
     wq,
     wk,
     wv,
@@ -101,25 +99,34 @@
     part_sems,
     text_back_sems,
     vis_back_sems,
+    weight_sems,
+    twin_sems,
 ):
     me = lax.axis_index("dp")
     core = lax.axis_index("tensor")
     other = 1 - core
     rows = text_buf.shape[1]
     text_half = rows // 2
-    cols = text_buf.shape[2]
+    cols = merger.shape[1]
     width = llm_gain.shape[1]
+    nz = n // 2
+    z, y = me // 2, lax.rem(me, 2)
+    mate = {"dp": me + 1 - 2 * y}
     sibling = {"tensor": other}
     kv = llm_k_hbm.shape[1]
 
     def ahead(step):
         return lax.rem(me + step, n)
 
-    def behind(step):
-        return lax.rem(me + n - step, n)
+    def z_ahead(step):
+        return lax.rem(z + step, nz)
+
+    def z_behind(step):
+        return lax.rem(z + nz - step, nz)
 
     mine = pl.ds(pl.multiple_of(core * text_half, text_half), text_half)
     theirs = pl.ds(pl.multiple_of(other * text_half, text_half), text_half)
+    own_weight = pl.ds(pl.multiple_of(y * cols, cols), cols)
     loads = [
         pltpu.make_async_copy(source, target, load_sem.at[i])
         for i, (source, target) in enumerate(
@@ -129,8 +136,8 @@
                 (vit_k_hbm, wk),
                 (vit_v_hbm, wv),
                 (vit_out_hbm, wo),
-                (llm_k_hbm, pair_weight.at[:, 0:kv]),
-                (llm_v_hbm, pair_weight.at[:, kv : 2 * kv]),
+                (llm_k_hbm, pair_weight.at[own_weight, 0:kv]),
+                (llm_v_hbm, pair_weight.at[own_weight, kv : 2 * kv]),
                 (merger_hbm, merger),
             ]
         )
@@ -158,13 +165,13 @@
         )
 
     def text_copy(step):
-        start = pl.multiple_of(ahead(step) * cols, cols)
-        return remote(
-            text_in.at[:, pl.ds(start, cols)],
+        start = pl.multiple_of(z_ahead(step) * 2 * cols, 2 * cols)
+        return remote(
+            text_in.at[:, pl.ds(start, 2 * cols)],
             text_buf.at[step, mine],
             text_sems.at[0, step],
             text_sems.at[1, step],
-            {"dp": ahead(step)},
+            {"dp": z_ahead(step) * 2 + y},
         )
 
     def forward_copy(step):
@@ -179,10 +186,28 @@
     def merged_copy(step):
         return remote(
             merged.at[0],
-            merged.at[step],
+            merged.at[2 * step],
             merged_sems.at[0, step],
             merged_sems.at[1, step],
-            {"dp": ahead(step)},
+            {"dp": z_ahead(step) * 2 + y},
+        )
+
+    def twin_copy(step):
+        return remote(
+            merged.at[2 * step],
+            merged.at[2 * step + 1],
+            twin_sems.at[0, step],
+            twin_sems.at[1, step],
+            mate,
+        )
+
+    def weight_copy():
+        return remote(
+            pair_weight.at[own_weight],
+            pair_weight.at[own_weight],
+            weight_sems.at[0],
+            weight_sems.at[1],
+            mate,
         )
 
     def text_back(step):
@@ -191,7 +216,7 @@
             text_recv.at[step],
             text_back_sems.at[0, step],
             text_back_sems.at[1, step],
-            {"dp": behind(step)},
+            {"dp": z_behind(step) * 2 + y},
         )
 
     def vis_back(step):
@@ -203,12 +228,14 @@
             {"dp": ahead(step)},
         )
 
-    def each(first, act):
+    def each(first, last, act):
         def run(step, carry):
             act(step)
             return carry
 
-        lax.fori_loop(first, n, run, 0)
+        lax.fori_loop(first, last, run, 0)
+
+    llm_gain[...] = llm_gain_flat[...].reshape(1, -1)
 
     loads[0].wait()
 
@@ -218,17 +245,40 @@
         return carry
 
     lax.fori_loop(0, text_half // 16, norm_rows, 0)
-    own_cols = pl.ds(pl.multiple_of(me * cols, cols), cols)
+    own_cols = pl.ds(pl.multiple_of(z * 2 * cols, 2 * cols), 2 * cols)
     text_buf[0, mine, :] = text_in[:, own_cols]
     pl.semaphore_wait(barrier, n)
-    each(1, lambda step: text_copy(step).start())
+    each(1, nz, lambda step: text_copy(step).start())
     forward_copy(0).start()
-
-    normed = layer_norm(patches[...], vit_gain[...]).astype(jnp.bfloat16)
+    loads[5].wait()
+    loads[6].wait()
+    weight_copy().start()
+
+    count = patches.shape[0]
+    quarter = count // 4
+
+    def token_of(place):
+        part_of = sum([(place >= j * quarter).astype(jnp.int32) for j in range(1, 4)])
+        return place - quarter * part_of, part_of
+
+    def image_at(place):
+        token, end, image = token_of(place)[0], 0, 0
+        for i in range(image_tokens.shape[1]):
+            end = end + image_tokens[0, i]
+            image = image + (token >= end).astype(jnp.int32)
+        return image
+
+    down = lax.broadcasted_iota(jnp.int32, (count, count), 0)
+    across = lax.broadcasted_iota(jnp.int32, (count, count), 1)
+    token, place = token_of(down)
+    chosen = jnp.where(across == 4 * token + place, 1.0, 0.0).astype(jnp.bfloat16)
+    ordered[...] = dot32(chosen, patches[...])
+
+    normed = layer_norm(ordered[...], vit_gain[...].reshape(1, -1)).astype(jnp.bfloat16)
     for load, weight, place in zip(loads[1:4], (wq, wk, wv), (query, keys, values)):
         load.wait()
         place[...] = dot32(normed, weight[...]).astype(jnp.bfloat16)
-    same = image_col[...] == image_row[...]
+    same = image_at(down) == image_at(across)
     mixed[...] = jnp.zeros_like(mixed)
     for head in range(query.shape[1] // VHD):
         low = head * VHD
@@ -253,37 +303,69 @@
     swap = remote(mix.at[other_half], mix_recv, mix_sems.at[0], mix_sems.at[1], sibling)
     swap.start()
     swap.wait()
-    hidden = (patches[own_half, :].astype(jnp.float32) + (mix[own_half, :] + mix_recv[...])).astype(
+    hidden = (ordered[own_half, :] + (mix[own_half, :] + mix_recv[...])).astype(
         jnp.bfloat16
     )
-    normal = layer_norm(hidden, merge_gain[...]).astype(jnp.bfloat16)
+    normal = layer_norm(hidden, merge_gain[...].reshape(1, -1)).astype(jnp.bfloat16)
     vision_width = normal.shape[1]
     merged[0, :, 0:vision_width] = normal[: half // 2]
     merged[0, :, vision_width : 2 * vision_width] = normal[half // 2 :]
-    each(1, lambda step: merged_copy(step).start())
+    each(1, nz, lambda step: merged_copy(step).start())
+    twin_copy(0).start()
+
+    slots = vis_send.shape[1]
+    per_block = code.shape[0] // n
+    capacity = slots // n
+    lanes = lax.broadcasted_iota(jnp.int32, (per_block, 128), 1)
+    before = jnp.where(
+        lax.broadcasted_iota(jnp.int32, (per_block, per_block), 1)
+        < lax.broadcasted_iota(jnp.int32, (per_block, per_block), 0),
+        1.0,
+        0.0,
+    ).astype(jnp.bfloat16)
+    slot_of = lax.broadcasted_iota(jnp.int32, (per_block, slots), 1) + me * slots
+
+    def place_block(i, total):
+        parity = lax.rem(i, 2)
+        source = z_behind(i // 2) * 2 + lax.rem(y + parity, 2)
+        at = pl.ds(pl.multiple_of(source * per_block, per_block), per_block)
+        owner = route[at, :]
+        onehot = jnp.where(lanes == owner, 1.0, 0.0)
+        earlier = dot32(before, onehot.astype(jnp.bfloat16))
+        rank = jnp.sum(earlier * onehot, axis=1, keepdims=True).astype(jnp.int32)
+        number = owner * slots + source * capacity + rank
+        code[pl.ds(pl.multiple_of(i * per_block, per_block), per_block), :] = number
+        named = jnp.where(number == slot_of, vis_seq[at, :] + 1, 0)
+        return total + jnp.sum(named, axis=0, keepdims=True)
+
+    marker[...] = lax.fori_loop(0, n, place_block, jnp.zeros((1, slots), jnp.int32))
 
     def hand_over(step):
         text_copy(step).wait_recv()
         forward_copy(step).start()
 
-    each(1, hand_over)
-    loads[5].wait()
-    loads[6].wait()
+    each(1, nz, hand_over)
+
+    def pass_on(step):
+        merged_copy(step).wait_recv()
+        twin_copy(step).start()
+
+    each(1, nz, pass_on)
+    weight_copy().wait_recv()
 
     def project_text(step):
         forward_copy(step).wait_recv()
         text_send[step] = dot32(text_buf[step], pair_weight[...]).astype(jnp.bfloat16)
 
-    project_text(0)
-
     def project_and_send(step):
         project_text(step)
         text_back(step).start()
 
-    each(1, project_and_send)
+    each(1, nz, project_and_send)
+    project_text(0)
 
     loads[7].wait()
-    each(1, lambda step: merged_copy(step).wait_recv())
+    each(0, nz, lambda step: twin_copy(step).wait_recv())
     gathered = merged[...].reshape(-1, merged.shape[2])
     block = 256
 
@@ -306,30 +388,34 @@
         wide = (part[:, at] + part_recv[:, at]).astype(jnp.bfloat16).astype(jnp.float32)
         power = power + jnp.sum(wide * wide, axis=1, keepdims=True)
         gain = llm_gain[:, pl.ds(pl.multiple_of(me * cols + i * block, block), block)]
-        pair = pair + dot32((wide * gain).astype(jnp.bfloat16), pair_weight[at, :])
+        weight = pair_weight[pl.ds(pl.multiple_of(y * cols + i * block, block), block), :]
+        pair = pair + dot32((wide * gain).astype(jnp.bfloat16), weight)
     coarse = power.astype(jnp.bfloat16).astype(jnp.float32)
     lane = lax.broadcasted_iota(jnp.int32, (tokens, MARK), 1)
     marks = jnp.where(lane < MARK // 2, coarse, power - coarse)
     row = jnp.concatenate([pair.astype(jnp.bfloat16), marks.astype(jnp.bfloat16)], axis=1)
 
-    def route(step):
-        vis_send[step] = dot32(selector[step], row).astype(jnp.bfloat16)
-
-    route(0)
+    def route_to(step):
+        wanted = lax.broadcasted_iota(jnp.int32, (tokens, slots), 1) + ahead(step) * slots
+        picked = jnp.where(code[...] == wanted, 1.0, 0.0).astype(jnp.bfloat16)
+        vis_send[step] = lax.dot_general(
+            picked, row, (((0,), (0,)), ((), ())), preferred_element_type=jnp.float32
+        ).astype(jnp.bfloat16)
+
+    route_to(0)
 
     def route_and_send(step):
-        route(step)
+        route_to(step)
         vis_back(step).start()
 
-    each(1, route_and_send)
-
-    slots = vis_send.shape[1]
+    each(1, n, route_and_send)
+
 
     def add_text(step, total):
         text_back(step).wait_recv()
         return total + text_recv[step].astype(jnp.float32)
 
-    out[slots:, :] = lax.fori_loop(1, n, add_text, text_send[0].astype(jnp.float32)).astype(
+    out[slots:, :] = lax.fori_loop(1, nz, add_text, text_send[0].astype(jnp.float32)).astype(
         jnp.bfloat16
     )
 
@@ -341,7 +427,9 @@
     squares = jnp.sum(total[:, 2 * kv :], axis=1, keepdims=True) * (2.0 / MARK)
     out[:slots, :] = (total[:, : 2 * kv] * lax.rsqrt(squares / width + EPSILON)).astype(jnp.bfloat16)
 
-    each(0, lambda step: forward_copy(step).wait_send())
+    each(0, nz, lambda step: forward_copy(step).wait_send())
+    each(0, nz, lambda step: twin_copy(step).wait_send())
+    weight_copy().wait_send()
     for i in range(cols // block):
         part_copy(i).wait_send()
 
@@ -349,9 +437,9 @@
         text_copy(step).wait_send()
         merged_copy(step).wait_send()
         text_back(step).wait_send()
-        vis_back(step).wait_send()
-
-    each(1, drain)
+
+    each(1, nz, drain)
+    each(1, n, lambda step: vis_back(step).wait_send())
 
 
 def body(
@@ -374,60 +462,40 @@
     llm_v,
 ):
     devices = lax.axis_size("dp")
-    dp_index = lax.axis_index("dp")
     total, width = patches.shape
-    ordered = patches.reshape(total // 4, 4, width).transpose(1, 0, 2).reshape(total, width)
-    image_of = image_index(image_tokens[0], total).reshape(total // 4, 4).T.reshape(total)
     key_cols = llm_k.shape[1]
-    owner_of = vis_route[:, 0]
-    token_count = owner_of.shape[0]
-    per_block = token_count // devices
-    capacity = 2 * per_block // devices
-    owner_slots = devices * capacity
-    ids = jnp.arange(devices, dtype=jnp.int32)
-    owners = owner_of.reshape(devices, per_block)
-    earlier = jnp.arange(per_block)[None, :] < jnp.arange(per_block)[:, None]
-    alike = (owners[:, :, None] == owners[:, None, :]) & earlier[None]
-    rank = jnp.sum(alike.astype(jnp.int32), axis=2)
-    local_slot = ids[:, None] * capacity + rank
-    slot_ids = jnp.arange(owner_slots, dtype=jnp.int32)
-    hits = (owner_of == dp_index)[None, :] & (slot_ids[:, None] == local_slot.reshape(-1)[None, :])
-    visual_marker = jnp.sum(jnp.where(hits, (vis_seq + 1)[None, :], 0), axis=1)
-    source = (dp_index - ids) % devices
-    turned_owner = jnp.sum(
-        jnp.where(source[:, None, None] == ids[None, :, None], owners[None], 0), axis=1
-    ).reshape(-1)
-    turned_slot = jnp.sum(
-        jnp.where(source[:, None, None] == ids[None, :, None], local_slot[None], 0), axis=1
-    ).reshape(-1)
-    target = (dp_index + ids) % devices
-    selector = (
-        (turned_owner[None, None, :] == target[:, None, None])
-        & (turned_slot[None, None, :] == slot_ids[None, :, None])
-    ).astype(jnp.bfloat16)
-
+    token_count = vis_route.shape[0]
+    owner_slots = 2 * token_count // devices
     text_count, model_width = text_rows.shape
     cols = merger_out.shape[1]
     half = total // 2
     vmem = pl.BlockSpec(memory_space=pltpu.VMEM)
+    smem = pl.BlockSpec(memory_space=pltpu.SMEM)
     hbm = pl.BlockSpec(memory_space=pl.ANY)
     bf16, f32 = jnp.bfloat16, jnp.float32
     dma = pltpu.SemaphoreType.DMA
-    pair = pl.pallas_call(
+    pairs = devices // 2
+    pair, visual_marker = pl.pallas_call(
         functools.partial(kernel, devices),
-        out_shape=jax.ShapeDtypeStruct((owner_slots + text_count, 2 * key_cols), bf16),
-        in_specs=[vmem] * 4 + [hbm] * 4 + [vmem, hbm, hbm, vmem, vmem, hbm, hbm],
-        out_specs=vmem,
+        out_shape=(
+            jax.ShapeDtypeStruct((owner_slots + text_count, 2 * key_cols), bf16),
+            jax.ShapeDtypeStruct((1, owner_slots), jnp.int32),
+        ),
+        in_specs=[vmem, smem, vmem] + [hbm] * 4 + [vmem, hbm, hbm, vmem, vmem, vmem, hbm, hbm],
+        out_specs=(vmem, vmem),
         scratch_shapes=[
+            pltpu.VMEM((token_count, 1), jnp.int32),
+            pltpu.VMEM((1, model_width), f32),
+            pltpu.VMEM((total, width), f32),
             pltpu.VMEM(vit_q.shape, bf16),
             pltpu.VMEM(vit_k.shape, bf16),
             pltpu.VMEM(vit_v.shape, bf16),
             pltpu.VMEM(vit_out.shape, bf16),
             pltpu.VMEM(merger_out.shape, bf16),
-            pltpu.VMEM((cols, 2 * key_cols), bf16),
+            pltpu.VMEM((2 * cols, 2 * key_cols), bf16),
             pltpu.VMEM((text_count // 2, model_width), bf16),
             pltpu.VMEM((text_count // 2, model_width), bf16),
-            pltpu.VMEM((devices, text_count, cols), bf16),
+            pltpu.VMEM((pairs, text_count, 2 * cols), bf16),
             pltpu.VMEM((total, vit_q.shape[1]), bf16),
             pltpu.VMEM((total, vit_q.shape[1]), bf16),
             pltpu.VMEM((total, vit_q.shape[1]), bf16),
@@ -437,8 +505,8 @@
             pltpu.VMEM((devices, half // 2, 2 * width), bf16),
             pltpu.VMEM((token_count, cols), f32),
             pltpu.VMEM((token_count, cols), f32),
-            pltpu.VMEM((devices, text_count, 2 * key_cols), bf16),
-            pltpu.VMEM((devices, text_count, 2 * key_cols), bf16),
+            pltpu.VMEM((pairs, text_count, 2 * key_cols), bf16),
+            pltpu.VMEM((pairs, text_count, 2 * key_cols), bf16),
             pltpu.VMEM((devices, owner_slots, 2 * key_cols + MARK), bf16),
             pltpu.VMEM((devices, owner_slots, 2 * key_cols + MARK), bf16),
             dma((8,)),
@@ -449,24 +517,26 @@
             dma((2, cols // 256)),
             dma((2, devices)),
             dma((2, devices)),
+            dma((2,)),
+            dma((2, pairs)),
         ],
         compiler_params=pltpu.CompilerParams(
             collective_id=0, has_side_effects=True, vmem_limit_bytes=56 * 1024 * 1024
         ),
     )(
-        ordered,
-        image_of[:, None],
-        image_of[None, :],
-        vit_gain[None],
+        patches,
+        image_tokens,
+        vit_gain,
         vit_q,
         vit_k,
         vit_v,
         vit_out,
-        merge_gain[None],
+        merge_gain,
         merger_out,
         text_rows,
-        selector,
-        llm_gain[None],
+        vis_route,
+        vis_seq[:, None],
+        llm_gain,
         llm_k,
         llm_v,
     )
@@ -475,7 +545,7 @@
     text_allowed = (segment[:, None] == segment[None, :]) & (
         positions[None, :] <= positions[:, None]
     )
-    visual_allowed = visual_marker[None, :] == (segment + 1)[:, None]
+    visual_allowed = visual_marker == (segment + 1)[:, None]
     allowed = jnp.concatenate([visual_allowed, text_allowed], axis=1)
     local_groups = key_cols // HD
     query_heads = text_query.reshape(text_count, local_groups, QH // KVH, HD)

time: 113 us -> 83.2 us (0.74)
  Pallas kernels: 94.4 us -> 74 us
  other arithmetic: 6.7 us -> 2.22 us
  local copies, waits for them, and re-layouts: 8.93 us -> 5.07 us
    pallas_call x1, Pallas kernels: 94.4 us -> 74 us  [body(): pl.pallas_call(functools.partial(kernel, devices), out_shape=(jax.ShapeDt...]
    reshape x3 -> x0, local copies, waits for them, and re-layouts: 1.9 us -> none  [the longest x2 1.81 us: body(): patches.reshape(total // 4, 4, width).transpose(1, 0, 2)]
    another operation x2 -> x0, local copies, waits for them, and re-layouts: 1.4 us -> none  [the longest x1 0.72 us: body(): image_of[:, None]]
    unnamed x1 -> x0, other arithmetic: 1.34 us -> none
    broadcast_in_dim x3 -> x1, local copies, waits for them, and re-layouts: 2.66 us -> 1.45 us  [body(): vis_seq[:, None]]
where the time goes in v2:
time: 83.2 us; the launch traced here: 82.3 us
  Pallas kernels  74 us (89%)
  local copies, waits for them, and re-layouts  5.07 us (6%)
  other arithmetic  2.22 us (3%)
  matrix products  1.01 us (1%)
    pallas_call x1, Pallas kernels, body(): pl.pallas_call(functools.partial(kernel, devices), out_shape=(jax.ShapeDt...  74 us

profile of v2, /device:TPU:13, one launch (start us, length us, event | category | flops | bytes accessed | tf_op | source)
XLA Modules:
  0.0 82.3 jit_solution(10948740105117798670)
XLA Ops:
  0.0 0.7 broadcast_add_fusion
  0.7 0.8 fusion.15
  1.5 1.5 %copy.23.route = s32[256,1]{1,0:T(8,128)} copy(s32[256,1]{0,1:T(1,128)} %param.29) | data formatting | bytes 2048 | tf_op args[12]
  3.0 1.5 %copy.24.vis_seq = s32[256,1]{1,0:T(8,128)} copy(s32[256,1]{0,1:T(1,128)} %bitcast.26) | data formatting | bytes 2048 | tf_op jit(solution)/shard_map/broadcast_in_dim | solution.py:538
  4.4 0.0 copy-start
  4.4 74.0 %shard_map.163 = (bf16[192,512]{1,0:T(8,128)(2,1)}, s32[1,64]{1,0:T(1,128)}) custom-call(bf16[128,1280]{1,0:T(8,128)(2,1)} %patches.1, s32[1,4]{1,0:T(1,128)} %image_tokens.1, f32[1280]{0:T(1024)} %vit_gain.1, bf16[1280,640]{1,0:T(8,128)(2,1)} %vit_q_hbm.1, bf16[1280,640]{1,0:T(8,128)(2,1)} %vit_k_hbm.1, bf16[1280,640]{1,0:T(8,128)(2,1)} %vit_v_hbm.1, ...), custom_call_target="tpu_custom_call" | custom-call | tf_op jit(solution)/shard_map/pallas_call | solution.py:478
  78.4 1.0 %fusion.18 = (bf16[192,256]{1,0:T(8,128)(2,1)S(1)}, bf16[192,256]{1,0:T(8,128)(2,1)S(1)}) fusion(bf16[192,512]{1,0:T(8,128)(2,1)} %get-tuple-element.7), kind=kLoop, calls=%fused_computation.18 | loop fusion | bytes 393216 | tf_op jit(solution)/shard_map/slice | solution.py:553
  79.4 0.7 broadcast_compare_fusion
  80.2 0.0 copy-done
  80.2 0.1 copy.35
  80.3 0.6 fusion.19
  81.0 0.4 convolution_convert_fusion
  81.3 1.0 %copy.28 = bf16[128,2048]{1,0:T(8,128)(2,1)} copy(bf16[128,2048]{0,1:T(8,128)(2,1)S(1)} %bitcast.22) | data formatting | bytes 1048576 | tf_op jit(solution)/shard_map/convert_element_type | solution.py:39
  (3 shorter events, 0.1 us)
Async XLA Ops:
  4.4 75.8 %copy-start = (bf16[128,2048]{1,0:T(8,128)(2,1)S(1)}, bf16[128,2048]{1,0:T(8,128)(2,1)}, u32[]{:S(2)}) copy-start(bf16[128,2048]{1,0:T(8,128)(2,1)} %param.27) | copy-start | bytes 1572868

commit v3 on v2

--- a/solution.py
+++ b/solution.py
@@ -23,12 +23,6 @@
     centred = values - jnp.mean(values, axis=-1, keepdims=True)
     spread = jnp.mean(centred * centred, axis=-1, keepdims=True)
     return centred * lax.rsqrt(spread + EPSILON) * scale_gain
-
-
-def rms_norm(values, scale_gain):
-    values = values.astype(jnp.float32)
-    power = jnp.mean(values * values, axis=-1, keepdims=True)
-    return values * lax.rsqrt(power + EPSILON) * scale_gain
 
 
 def local_attention(query, keys, values, allowed, scale):
@@ -76,7 +70,9 @@
     merger,
     pair_weight,
     text,
-    text_in,
+    text_scale,
+    route_wide,
+    seq_wide,
     text_buf,
     query,
     keys,
@@ -88,9 +84,13 @@
     part,
     part_recv,
     text_send,
+    text_sum,
     text_recv,
     vis_send,
     vis_recv,
+    vis_mate,
+    vis_mate_recv,
+    vis_sum,
     load_sem,
     text_sems,
     forward_sems,
@@ -101,6 +101,7 @@
     vis_back_sems,
     weight_sems,
     twin_sems,
+    mate_sems,
 ):
     me = lax.axis_index("dp")
     core = lax.axis_index("tensor")
@@ -115,9 +116,6 @@
     sibling = {"tensor": other}
     kv = llm_k_hbm.shape[1]
 
-    def ahead(step):
-        return lax.rem(me + step, n)
-
     def z_ahead(step):
         return lax.rem(z + step, nz)
 
@@ -131,7 +129,7 @@
         pltpu.make_async_copy(source, target, load_sem.at[i])
         for i, (source, target) in enumerate(
             [
-                (text_hbm.at[mine], text),
+                (text_hbm, text),
                 (vit_q_hbm, wq),
                 (vit_k_hbm, wk),
                 (vit_v_hbm, wv),
@@ -148,10 +146,12 @@
     barrier = pltpu.get_barrier_semaphore()
 
     def greet(step, carry):
-        pl.semaphore_signal(barrier, inc=1, device_id={"dp": ahead(step)}, device_id_type=MESH)
+        peer = {"dp": z_ahead(step) * 2 + y}
+        pl.semaphore_signal(barrier, inc=1, device_id=peer, device_id_type=MESH)
         return carry
 
-    lax.fori_loop(1, n, greet, 0)
+    lax.fori_loop(1, nz, greet, 0)
+    pl.semaphore_signal(barrier, inc=1, device_id=mate, device_id_type=MESH)
     pl.semaphore_signal(barrier, inc=1, device_id=sibling, device_id_type=MESH)
 
     def remote(source, target, send, recv, device):
@@ -167,7 +167,7 @@
     def text_copy(step):
         start = pl.multiple_of(z_ahead(step) * 2 * cols, 2 * cols)
         return remote(
-            text_in.at[:, pl.ds(start, 2 * cols)],
+            text_hbm.at[mine, pl.ds(start, 2 * cols)],
             text_buf.at[step, mine],
             text_sems.at[0, step],
             text_sems.at[1, step],
@@ -225,7 +225,16 @@
             vis_recv.at[step],
             vis_back_sems.at[0, step],
             vis_back_sems.at[1, step],
-            {"dp": ahead(step)},
+            {"dp": z_ahead(step) * 2 + y},
+        )
+
+    def mate_copy(step):
+        return remote(
+            vis_mate.at[step],
+            vis_mate_recv.at[step],
+            mate_sems.at[0, step],
+            mate_sems.at[1, step],
+            mate,
         )
 
     def each(first, last, act):
@@ -237,19 +246,11 @@
 
     llm_gain[...] = llm_gain_flat[...].reshape(1, -1)
 
-    loads[0].wait()
-
-    def norm_rows(i, carry):
-        at = pl.ds(pl.multiple_of(i * 16, 16), 16)
-        text_in[at, :] = rms_norm(text[at, :], llm_gain[...]).astype(jnp.bfloat16)
-        return carry
-
-    lax.fori_loop(0, text_half // 16, norm_rows, 0)
     own_cols = pl.ds(pl.multiple_of(z * 2 * cols, 2 * cols), 2 * cols)
-    text_buf[0, mine, :] = text_in[:, own_cols]
-    pl.semaphore_wait(barrier, n)
+    own_text = pltpu.make_async_copy(text_hbm.at[:, own_cols], text_buf.at[0], load_sem.at[8])
+    own_text.start()
+    pl.semaphore_wait(barrier, nz + 1)
     each(1, nz, lambda step: text_copy(step).start())
-    forward_copy(0).start()
     loads[5].wait()
     loads[6].wait()
     weight_copy().start()
@@ -313,6 +314,12 @@
     each(1, nz, lambda step: merged_copy(step).start())
     twin_copy(0).start()
 
+    route_wide[...] = jnp.broadcast_to(
+        route[...].astype(jnp.float32).reshape(1, -1), (128, code.shape[0])
+    ).T
+    seq_wide[...] = jnp.broadcast_to(
+        vis_seq[...].astype(jnp.float32).reshape(1, -1), (128, code.shape[0])
+    ).T
     slots = vis_send.shape[1]
     per_block = code.shape[0] // n
     capacity = slots // n
@@ -329,13 +336,13 @@
         parity = lax.rem(i, 2)
         source = z_behind(i // 2) * 2 + lax.rem(y + parity, 2)
         at = pl.ds(pl.multiple_of(source * per_block, per_block), per_block)
-        owner = route[at, :]
+        owner = route_wide[at, :].astype(jnp.int32)
         onehot = jnp.where(lanes == owner, 1.0, 0.0)
         earlier = dot32(before, onehot.astype(jnp.bfloat16))
         rank = jnp.sum(earlier * onehot, axis=1, keepdims=True).astype(jnp.int32)
-        number = owner * slots + source * capacity + rank
+        number = owner[:, 0:1] * slots + source * capacity + rank
         code[pl.ds(pl.multiple_of(i * per_block, per_block), per_block), :] = number
-        named = jnp.where(number == slot_of, vis_seq[at, :] + 1, 0)
+        named = jnp.where(number == slot_of, seq_wide[at, 0:slots].astype(jnp.int32) + 1, 0)
         return total + jnp.sum(named, axis=0, keepdims=True)
 
     marker[...] = lax.fori_loop(0, n, place_block, jnp.zeros((1, slots), jnp.int32))
@@ -344,6 +351,18 @@
         text_copy(step).wait_recv()
         forward_copy(step).start()
 
+    loads[0].wait()
+
+    def scale_rows(i, carry):
+        at = pl.ds(pl.multiple_of(i * 16, 16), 16)
+        wide = text[at, :].astype(jnp.float32)
+        squares = jnp.sum(wide * wide, axis=1, keepdims=True)
+        text_scale[at, :] = jnp.broadcast_to(
+            lax.rsqrt(squares / width + EPSILON), (16, text_scale.shape[1])
+        )
+        return carry
+
+    lax.fori_loop(0, rows // 16, scale_rows, 0)
     each(1, nz, hand_over)
 
     def pass_on(step):
@@ -354,15 +373,17 @@
     weight_copy().wait_recv()
 
     def project_text(step):
+        gained = (text_buf[step].astype(jnp.float32) * llm_gain[:, own_cols]).astype(jnp.bfloat16)
+        return dot32(gained, pair_weight[...])
+
+    def project_and_send(step):
         forward_copy(step).wait_recv()
-        text_send[step] = dot32(text_buf[step], pair_weight[...]).astype(jnp.bfloat16)
-
-    def project_and_send(step):
-        project_text(step)
+        text_send[step] = project_text(step).astype(jnp.bfloat16)
         text_back(step).start()
 
     each(1, nz, project_and_send)
-    project_text(0)
+    own_text.wait()
+    text_sum[...] = project_text(0)
 
     loads[7].wait()
     each(0, nz, lambda step: twin_copy(step).wait_recv())
@@ -390,44 +411,59 @@
         gain = llm_gain[:, pl.ds(pl.multiple_of(me * cols + i * block, block), block)]
         weight = pair_weight[pl.ds(pl.multiple_of(y * cols + i * block, block), block), :]
         pair = pair + dot32((wide * gain).astype(jnp.bfloat16), weight)
-    coarse = power.astype(jnp.bfloat16).astype(jnp.float32)
-    lane = lax.broadcasted_iota(jnp.int32, (tokens, MARK), 1)
-    marks = jnp.where(lane < MARK // 2, coarse, power - coarse)
-    row = jnp.concatenate([pair.astype(jnp.bfloat16), marks.astype(jnp.bfloat16)], axis=1)
-
-    def route_to(step):
-        wanted = lax.broadcasted_iota(jnp.int32, (tokens, slots), 1) + ahead(step) * slots
+
+    def marked(square):
+        coarse = square.astype(jnp.bfloat16).astype(jnp.float32)
+        lane = lax.broadcasted_iota(jnp.int32, (square.shape[0], MARK), 1)
+        return jnp.where(lane < MARK // 2, coarse, square - coarse).astype(jnp.bfloat16)
+
+    row = jnp.concatenate([pair.astype(jnp.bfloat16), marked(power)], axis=1)
+
+    def route_to(owner):
+        wanted = lax.broadcasted_iota(jnp.int32, (tokens, slots), 1) + owner * slots
         picked = jnp.where(code[...] == wanted, 1.0, 0.0).astype(jnp.bfloat16)
-        vis_send[step] = lax.dot_general(
+        return lax.dot_general(
             picked, row, (((0,), (0,)), ((), ())), preferred_element_type=jnp.float32
-        ).astype(jnp.bfloat16)
-
-    route_to(0)
+        )
+
+    def route_for_mate(step):
+        vis_mate[step] = route_to(z_ahead(step) * 2 + 1 - y).astype(jnp.bfloat16)
+        mate_copy(step).start()
+
+    def route_own(step):
+        total = route_to(z_ahead(step) * 2 + y)
+        mate_copy(step).wait_recv()
+        return total + vis_mate_recv[step].astype(jnp.float32)
 
     def route_and_send(step):
-        route_to(step)
+        total = route_own(step)
+        square = jnp.sum(total[:, 2 * kv :], axis=1, keepdims=True) * (2.0 / MARK)
+        vis_send[step, :, 0 : 2 * kv] = total[:, : 2 * kv].astype(jnp.bfloat16)
+        vis_send[step, :, 2 * kv :] = marked(square)
         vis_back(step).start()
 
-    each(1, n, route_and_send)
+    each(1, nz, route_for_mate)
+    route_for_mate(0)
+    each(1, nz, route_and_send)
+    vis_sum[...] = route_own(0)
 
 
     def add_text(step, total):
         text_back(step).wait_recv()
         return total + text_recv[step].astype(jnp.float32)
 
-    out[slots:, :] = lax.fori_loop(1, nz, add_text, text_send[0].astype(jnp.float32)).astype(
-        jnp.bfloat16
-    )
+    text_total = lax.fori_loop(1, nz, add_text, text_sum[...])
+    out[slots:, :] = (text_total * text_scale[:, 0:1]).astype(jnp.bfloat16)
 
     def add_visual(step, total):
         vis_back(step).wait_recv()
         return total + vis_recv[step].astype(jnp.float32)
 
-    total = lax.fori_loop(1, n, add_visual, vis_send[0].astype(jnp.float32))
+    total = lax.fori_loop(1, nz, add_visual, vis_sum[...])
     squares = jnp.sum(total[:, 2 * kv :], axis=1, keepdims=True) * (2.0 / MARK)
     out[:slots, :] = (total[:, : 2 * kv] * lax.rsqrt(squares / width + EPSILON)).astype(jnp.bfloat16)
 
-    each(0, nz, lambda step: forward_copy(step).wait_send())
+    each(1, nz, lambda step: forward_copy(step).wait_send())
     each(0, nz, lambda step: twin_copy(step).wait_send())
     weight_copy().wait_send()
     for i in range(cols // block):
@@ -439,7 +475,8 @@
         text_back(step).wait_send()
 
     each(1, nz, drain)
-    each(1, n, lambda step: vis_back(step).wait_send())
+    each(1, nz, lambda step: vis_back(step).wait_send())
+    each(0, nz, lambda step: mate_copy(step).wait_send())
 
 
 def body(
@@ -493,8 +530,10 @@
             pltpu.VMEM(vit_out.shape, bf16),
             pltpu.VMEM(merger_out.shape, bf16),
             pltpu.VMEM((2 * cols, 2 * key_cols), bf16),
-            pltpu.VMEM((text_count // 2, model_width), bf16),
-            pltpu.VMEM((text_count // 2, model_width), bf16),
+            pltpu.VMEM((text_count, model_width), bf16),
+            pltpu.VMEM((text_count, 128), f32),
+            pltpu.VMEM((token_count, 128), f32),
+            pltpu.VMEM((token_count, 128), f32),
             pltpu.VMEM((pairs, text_count, 2 * cols), bf16),
             pltpu.VMEM((total, vit_q.shape[1]), bf16),
             pltpu.VMEM((total, vit_q.shape[1]), bf16),
@@ -506,10 +545,14 @@
             pltpu.VMEM((token_count, cols), f32),
             pltpu.VMEM((token_count, cols), f32),
             pltpu.VMEM((pairs, text_count, 2 * key_cols), bf16),
+            pltpu.VMEM((text_count, 2 * key_cols), f32),
             pltpu.VMEM((pairs, text_count, 2 * key_cols), bf16),
-            pltpu.VMEM((devices, owner_slots, 2 * key_cols + MARK), bf16),
-            pltpu.VMEM((devices, owner_slots, 2 * key_cols + MARK), bf16),
-            dma((8,)),
+            pltpu.VMEM((pairs, owner_slots, 2 * key_cols + MARK), bf16),
+            pltpu.VMEM((pairs, owner_slots, 2 * key_cols + MARK), bf16),
+            pltpu.VMEM((pairs, owner_slots, 2 * key_cols + MARK), bf16),
+            pltpu.VMEM((pairs, owner_slots, 2 * key_cols + MARK), bf16),
+            pltpu.VMEM((owner_slots, 2 * key_cols + MARK), f32),
+            dma((9,)),
             dma((2, devices)),
             dma((2, devices)),
             dma((2,)),
@@ -518,6 +561,7 @@
             dma((2, devices)),
             dma((2, devices)),
             dma((2,)),
+            dma((2, pairs)),
             dma((2, pairs)),
         ],
         compiler_params=pltpu.CompilerParams(
@@ -534,8 +578,8 @@
         merge_gain,
         merger_out,
         text_rows,
-        vis_route,
-        vis_seq[:, None],
+        vis_route.reshape(-1),
+        vis_seq,
         llm_gain,
         llm_k,
         llm_v,

time: 83.2 us -> 78.9 us (0.948)
  local copies, waits for them, and re-layouts: 5.07 us -> 2.14 us
  Pallas kernels: 74 us -> 72.3 us
    pallas_call x1, Pallas kernels: 74 us -> 72.3 us  [body(): pl.pallas_call(functools.partial(kernel, devices), out_shape=(jax.ShapeDt...]
    unnamed x4 -> x3, local copies, waits for them, and re-layouts: 1.59 us -> 0.12 us
    broadcast_in_dim x1 -> x0, local copies, waits for them, and re-layouts: 1.45 us -> none  [body(): vis_seq[:, None]]
where the time goes in v3:
time: 78.9 us; the launch traced here: 77.7 us
  Pallas kernels  72.3 us (92%)
  other arithmetic  2.21 us (3%)
  local copies, waits for them, and re-layouts  2.14 us (3%)
  matrix products  1 us (1%)
    pallas_call x1, Pallas kernels, body(): pl.pallas_call(functools.partial(kernel, devices), out_shape=(jax.ShapeDt...  72.3 us

profile of v3, /device:TPU:13, one launch (start us, length us, event | category | flops | bytes accessed | tf_op | source)
XLA Modules:
  0.0 77.7 jit_solution(6076491546771987757)
XLA Ops:
  0.0 0.7 broadcast_add_fusion
  0.7 0.8 %fusion.15 = pred[128,128]{0,1:T(8,128)(4,1)S(1)} fusion(s32[128]{0:T(128)} %bitcast.25), kind=kLoop, calls=%fused_computation.13 | loop fusion | flops 49152 | bytes 16896 | tf_op jit(solution)/shard_map/and | solution.py:589
  1.5 0.0 copy-start
  1.5 72.3 %shard_map.163 = (bf16[192,512]{1,0:T(8,128)(2,1)}, s32[1,64]{1,0:T(1,128)}) custom-call(bf16[128,1280]{1,0:T(8,128)(2,1)} %patches.1, s32[1,4]{1,0:T(1,128)} %image_tokens.1, f32[1280]{0:T(1024)} %vit_gain.1, bf16[1280,640]{1,0:T(8,128)(2,1)} %vit_q_hbm.1, bf16[1280,640]{1,0:T(8,128)(2,1)} %vit_k_hbm.1, bf16[1280,640]{1,0:T(8,128)(2,1)} %vit_v_hbm.1, ...), custom_call_target="tpu_custom_call" | custom-call | tf_op jit(solution)/shard_map/pallas_call | solution.py:515
  73.8 1.0 %fusion.18 = (bf16[192,256]{1,0:T(8,128)(2,1)S(1)}, bf16[192,256]{1,0:T(8,128)(2,1)S(1)}) fusion(bf16[192,512]{1,0:T(8,128)(2,1)} %get-tuple-element.7), kind=kLoop, calls=%fused_computation.18 | loop fusion | bytes 393216 | tf_op jit(solution)/shard_map/slice | solution.py:597
  74.8 0.7 broadcast_compare_fusion
  75.6 0.0 copy-done
  75.6 0.1 copy.28
  75.7 0.6 fusion.19
  76.3 0.4 convolution_convert_fusion
  76.7 1.0 %copy.21 = bf16[128,2048]{1,0:T(8,128)(2,1)} copy(bf16[128,2048]{0,1:T(8,128)(2,1)S(1)} %bitcast.22) | data formatting | bytes 1048576 | tf_op jit(solution)/shard_map/convert_element_type | solution.py:33
  (3 shorter events, 0.1 us)
Async XLA Ops:
  1.5 74.1 %copy-start = (bf16[128,2048]{1,0:T(8,128)(2,1)S(1)}, bf16[128,2048]{1,0:T(8,128)(2,1)}, u32[]{:S(2)}) copy-start(bf16[128,2048]{1,0:T(8,128)(2,1)} %param.27) | copy-start | bytes 1572868

commit v4 on v3

--- a/solution.py
+++ b/solution.py
@@ -183,30 +183,37 @@
             sibling,
         )
 
-    def merged_copy(step):
-        return remote(
-            merged.at[0],
-            merged.at[2 * step],
-            merged_sems.at[0, step],
-            merged_sems.at[1, step],
+    chunk = merged.shape[1] // 2
+
+    def merged_copy(index):
+        step = index // 2
+        at = pl.ds(pl.multiple_of(lax.rem(index, 2) * chunk, chunk), chunk)
+        return remote(
+            merged.at[0, at],
+            merged.at[2 * step, at],
+            merged_sems.at[0, index],
+            merged_sems.at[1, index],
             {"dp": z_ahead(step) * 2 + y},
         )
 
-    def twin_copy(step):
-        return remote(
-            merged.at[2 * step],
-            merged.at[2 * step + 1],
-            twin_sems.at[0, step],
-            twin_sems.at[1, step],
+    def twin_copy(index):
+        step = index // 2
+        at = pl.ds(pl.multiple_of(lax.rem(index, 2) * chunk, chunk), chunk)
+        return remote(
+            merged.at[2 * step, at],
+            merged.at[2 * step + 1, at],
+            twin_sems.at[0, index],
+            twin_sems.at[1, index],
             mate,
         )
 
-    def weight_copy():
-        return remote(
-            pair_weight.at[own_weight],
-            pair_weight.at[own_weight],
-            weight_sems.at[0],
-            weight_sems.at[1],
+    def weight_copy(i):
+        piece = pair_weight.at[own_weight, i * kv : (i + 1) * kv]
+        return remote(
+            piece,
+            piece,
+            weight_sems.at[0, i],
+            weight_sems.at[1, i],
             mate,
         )
 
@@ -250,10 +257,9 @@
     own_text = pltpu.make_async_copy(text_hbm.at[:, own_cols], text_buf.at[0], load_sem.at[8])
     own_text.start()
     pl.semaphore_wait(barrier, nz + 1)
-    each(1, nz, lambda step: text_copy(step).start())
+    text_copy(nz // 2).start()
     loads[5].wait()
-    loads[6].wait()
-    weight_copy().start()
+    weight_copy(0).start()
 
     count = patches.shape[0]
     quarter = count // 4
@@ -311,8 +317,11 @@
     vision_width = normal.shape[1]
     merged[0, :, 0:vision_width] = normal[: half // 2]
     merged[0, :, vision_width : 2 * vision_width] = normal[half // 2 :]
-    each(1, nz, lambda step: merged_copy(step).start())
-    twin_copy(0).start()
+    each(1, nz, lambda step: merged_copy(2 * step).start())
+    each(1, nz, lambda step: merged_copy(2 * step + 1).start())
+    each(0, 2, lambda index: twin_copy(index).start())
+    each(1, nz // 2, lambda step: text_copy(step).start())
+    each(nz // 2 + 1, nz, lambda step: text_copy(step).start())
 
     route_wide[...] = jnp.broadcast_to(
         route[...].astype(jnp.float32).reshape(1, -1), (128, code.shape[0])
@@ -363,30 +372,19 @@
         return carry
 
     lax.fori_loop(0, rows // 16, scale_rows, 0)
-    each(1, nz, hand_over)
-
-    def pass_on(step):
-        merged_copy(step).wait_recv()
-        twin_copy(step).start()
-
-    each(1, nz, pass_on)
-    weight_copy().wait_recv()
-
-    def project_text(step):
-        gained = (text_buf[step].astype(jnp.float32) * llm_gain[:, own_cols]).astype(jnp.bfloat16)
-        return dot32(gained, pair_weight[...])
-
-    def project_and_send(step):
-        forward_copy(step).wait_recv()
-        text_send[step] = project_text(step).astype(jnp.bfloat16)
-        text_back(step).start()
-
-    each(1, nz, project_and_send)
-    own_text.wait()
-    text_sum[...] = project_text(0)
+
+    def pass_on(index):
+        merged_copy(index).wait_recv()
+        twin_copy(index).start()
+
+    each(1, nz, lambda step: pass_on(2 * step))
+    each(1, nz, lambda step: pass_on(2 * step + 1))
+    loads[6].wait()
+    weight_copy(1).start()
+    hand_over(nz // 2)
 
     loads[7].wait()
-    each(0, nz, lambda step: twin_copy(step).wait_recv())
+    each(0, 2 * nz, lambda index: twin_copy(index).wait_recv())
     gathered = merged[...].reshape(-1, merged.shape[2])
     block = 256
 
@@ -444,7 +442,26 @@
 
     each(1, nz, route_for_mate)
     route_for_mate(0)
+    each(1, nz // 2, hand_over)
+    each(nz // 2 + 1, nz, hand_over)
     each(1, nz, route_and_send)
+    weight_copy(0).wait_recv()
+    weight_copy(1).wait_recv()
+
+    def project_text(step):
+        gained = (text_buf[step].astype(jnp.float32) * llm_gain[:, own_cols]).astype(jnp.bfloat16)
+        return dot32(gained, pair_weight[...])
+
+    def project_and_send(step):
+        forward_copy(step).wait_recv()
+        text_send[step] = project_text(step).astype(jnp.bfloat16)
+        text_back(step).start()
+
+    project_and_send(nz // 2)
+    each(1, nz // 2, project_and_send)
+    each(nz // 2 + 1, nz, project_and_send)
+    own_text.wait()
+    text_sum[...] = project_text(0)
     vis_sum[...] = route_own(0)
 
 
@@ -464,14 +481,16 @@
     out[:slots, :] = (total[:, : 2 * kv] * lax.rsqrt(squares / width + EPSILON)).astype(jnp.bfloat16)
 
     each(1, nz, lambda step: forward_copy(step).wait_send())
-    each(0, nz, lambda step: twin_copy(step).wait_send())
-    weight_copy().wait_send()
+    each(0, 2 * nz, lambda index: twin_copy(index).wait_send())
+    weight_copy(0).wait_send()
+    weight_copy(1).wait_send()
     for i in range(cols // block):
         part_copy(i).wait_send()
 
     def drain(step):
         text_copy(step).wait_send()
-        merged_copy(step).wait_send()
+        merged_copy(2 * step).wait_send()
+        merged_copy(2 * step + 1).wait_send()
         text_back(step).wait_send()
 
     each(1, nz, drain)
@@ -556,12 +575,12 @@
             dma((2, devices)),
             dma((2, devices)),
             dma((2,)),
-            dma((2, devices)),
+            dma((2, 2 * pairs)),
             dma((2, cols // 256)),
             dma((2, devices)),
             dma((2, devices)),
-            dma((2,)),
-            dma((2, pairs)),
+            dma((2, 2)),
+            dma((2, 2 * pairs)),
             dma((2, pairs)),
         ],
         compiler_params=pltpu.CompilerParams(

time: 78.9 us -> 81.9 us (1.038); the launches traced: 77.7 us -> 81.8 us
  Pallas kernels: 72.3 us -> 76.3 us
    pallas_call x1, Pallas kernels: 72.3 us -> 76.3 us  [body(): pl.pallas_call(functools.partial(kernel, devices), out_shape=(jax.ShapeDt...]
where the time goes in v4:
time: 81.9 us; the launch traced here: 81.8 us
  Pallas kernels  76.3 us (93%)
  other arithmetic  2.21 us (3%)
  local copies, waits for them, and re-layouts  2.14 us (3%)
  matrix products  1 us (1%)
    pallas_call x1, Pallas kernels, body(): pl.pallas_call(functools.partial(kernel, devices), out_shape=(jax.ShapeDt...  76.3 us

profile of v4, /device:TPU:13, one launch (start us, length us, event | category | flops | bytes accessed | tf_op | source)
XLA Modules:
  0.0 81.8 jit_solution(11874540007237979799)
XLA Ops:
  0.0 0.7 broadcast_add_fusion
  0.7 0.8 fusion.15
  1.5 0.0 copy-start
  1.5 76.3 %shard_map.163 = (bf16[192,512]{1,0:T(8,128)(2,1)}, s32[1,64]{1,0:T(1,128)}) custom-call(bf16[128,1280]{1,0:T(8,128)(2,1)} %patches.1, s32[1,4]{1,0:T(1,128)} %image_tokens.1, f32[1280]{0:T(1024)} %vit_gain.1, bf16[1280,640]{1,0:T(8,128)(2,1)} %vit_q_hbm.1, bf16[1280,640]{1,0:T(8,128)(2,1)} %vit_k_hbm.1, bf16[1280,640]{1,0:T(8,128)(2,1)} %vit_v_hbm.1, ...), custom_call_target="tpu_custom_call" | custom-call | tf_op jit(solution)/shard_map/pallas_call | solution.py:534
  77.8 1.0 %fusion.18 = (bf16[192,256]{1,0:T(8,128)(2,1)S(1)}, bf16[192,256]{1,0:T(8,128)(2,1)S(1)}) fusion(bf16[192,512]{1,0:T(8,128)(2,1)} %get-tuple-element.7), kind=kLoop, calls=%fused_computation.18 | loop fusion | bytes 393216 | tf_op jit(solution)/shard_map/slice | solution.py:616
  78.8 0.7 broadcast_compare_fusion
  79.6 0.0 copy-done
  79.6 0.1 copy.28
  79.7 0.6 fusion.19
  80.4 0.4 convolution_convert_fusion
  80.7 1.0 %copy.21 = bf16[128,2048]{1,0:T(8,128)(2,1)} copy(bf16[128,2048]{0,1:T(8,128)(2,1)S(1)} %bitcast.22) | data formatting | bytes 1048576 | tf_op jit(solution)/shard_map/convert_element_type | solution.py:33
  (3 shorter events, 0.1 us)
Async XLA Ops:
  1.5 78.1 %copy-start = (bf16[128,2048]{1,0:T(8,128)(2,1)S(1)}, bf16[128,2048]{1,0:T(8,128)(2,1)}, u32[]{:S(2)}) copy-start(bf16[128,2048]{1,0:T(8,128)(2,1)} %param.27) | copy-start | bytes 1572868

commit v5 on v3

--- a/solution.py
+++ b/solution.py
@@ -363,13 +363,13 @@
         return carry
 
     lax.fori_loop(0, rows // 16, scale_rows, 0)
-    each(1, nz, hand_over)
 
     def pass_on(step):
         merged_copy(step).wait_recv()
         twin_copy(step).start()
 
     each(1, nz, pass_on)
+    each(1, nz, hand_over)
     weight_copy().wait_recv()
 
     def project_text(step):

time: 78.9 us -> 77.2 us (0.978)
  Pallas kernels: 72.3 us -> 71.1 us
    pallas_call x1, Pallas kernels: 72.3 us -> 71.1 us  [body(): pl.pallas_call(functools.partial(kernel, devices), out_shape=(jax.ShapeDt...]
where the time goes in v5:
time: 77.2 us; the launch traced here: 76.5 us
  Pallas kernels  71.1 us (92%)
  other arithmetic  2.21 us (3%)
  local copies, waits for them, and re-layouts  2.14 us (3%)
  matrix products  1.01 us (1%)
    pallas_call x1, Pallas kernels, body(): pl.pallas_call(functools.partial(kernel, devices), out_shape=(jax.ShapeDt...  71.1 us

profile of v5, /device:TPU:13, one launch (start us, length us, event | category | flops | bytes accessed | tf_op | source)
XLA Modules:
  0.0 76.5 jit_solution(13143023862056385535)
XLA Ops:
  0.0 0.7 broadcast_add_fusion
  0.7 0.8 %fusion.15 = pred[128,128]{0,1:T(8,128)(4,1)S(1)} fusion(s32[128]{0:T(128)} %bitcast.25), kind=kLoop, calls=%fused_computation.13 | loop fusion | flops 49152 | bytes 16896 | tf_op jit(solution)/shard_map/and | solution.py:589
  1.5 0.0 copy-start
  1.5 71.1 %shard_map.163 = (bf16[192,512]{1,0:T(8,128)(2,1)}, s32[1,64]{1,0:T(1,128)}) custom-call(bf16[128,1280]{1,0:T(8,128)(2,1)} %patches.1, s32[1,4]{1,0:T(1,128)} %image_tokens.1, f32[1280]{0:T(1024)} %vit_gain.1, bf16[1280,640]{1,0:T(8,128)(2,1)} %vit_q_hbm.1, bf16[1280,640]{1,0:T(8,128)(2,1)} %vit_k_hbm.1, bf16[1280,640]{1,0:T(8,128)(2,1)} %vit_v_hbm.1, ...), custom_call_target="tpu_custom_call" | custom-call | tf_op jit(solution)/shard_map/pallas_call | solution.py:515
  72.6 1.0 %fusion.18 = (bf16[192,256]{1,0:T(8,128)(2,1)S(1)}, bf16[192,256]{1,0:T(8,128)(2,1)S(1)}) fusion(bf16[192,512]{1,0:T(8,128)(2,1)} %get-tuple-element.7), kind=kLoop, calls=%fused_computation.18 | loop fusion | bytes 393216 | tf_op jit(solution)/shard_map/slice | solution.py:597
  73.6 0.7 broadcast_compare_fusion
  74.4 0.0 copy-done
  74.4 0.1 copy.28
  74.5 0.6 fusion.19
  75.2 0.4 convolution_convert_fusion
  75.5 1.0 %copy.21 = bf16[128,2048]{1,0:T(8,128)(2,1)} copy(bf16[128,2048]{0,1:T(8,128)(2,1)S(1)} %bitcast.22) | data formatting | bytes 1048576 | tf_op jit(solution)/shard_map/convert_element_type | solution.py:33
  (3 shorter events, 0.1 us)
Async XLA Ops:
  1.5 72.9 %copy-start = (bf16[128,2048]{1,0:T(8,128)(2,1)S(1)}, bf16[128,2048]{1,0:T(8,128)(2,1)}, u32[]{:S(2)}) copy-start(bf16[128,2048]{1,0:T(8,128)(2,1)} %param.27) | copy-start | bytes 1572868
